TPU v7x, 32 devices: a whole 2x2x4 slice. The times are simulated.
32 devices in a mesh: ens: 2 (over y), comp: 4 (over z), tile: 2 (over x), sub: 2 (over core).
Axes of the slice: x: 2, y: 2, z: 4, core: 2. Of those that a mesh axis runs over, the one named last changes fastest.
Arguments:
- spectrum: bfloat16 [4, 8, 1296, 256], P(('ens', 'tile'), ('comp', 'sub')), parts along dimension 0, may hold values from 0.03 to 15, as said below
- wind_speed: float32 [4, 8, 256], P(('ens', 'tile'), ('comp', 'sub')), parts along dimension 0, may hold values from 2 to 25
- wind_dir: float32 [4, 8, 256], P(('ens', 'tile'), ('comp', 'sub')), parts along dimension 0, may hold values from -3.140625 to 3.140625
- freq_kernel: float32 [36, 36], replicated, may hold values from -1 to 1
- dir_kernel: float32 [36, 36], replicated, may hold values from -1 to 1
- depth: float32 [32, 128], P('tile'), may hold values from 10 to 4000
- current: float32 [2, 32, 128], P(None, 'tile'), may hold values from -3 to 3
- land_mask: int32 [32, 128], P('tile'), may hold values from 0 to 1, as said below
- tile_owner: int32 [2, 32], P('tile'), may hold values from 0 to 7, as said below
Outputs:
- spectrum_out: bfloat16 [4, 8, 1296, 256], P(('ens', 'tile'), ('comp', 'sub')), parts along dimension 0
There are 2 independent parts, one for each index of `ens`. A program takes and returns all parts, laid end to end along the dimension named above; an argument that names none is the same for every part. Nothing has to cross between parts.
Inputs may be any that keep to these rules, and one draw needn't show every extreme that they name: `spectrum`: Positive. `land_mask`: 1 marks sea, 0 land. In every strip the busiest owner holds exactly 256 sea cells. `tile_owner`: in every strip each owner number appears exactly 4 times.
All inputs are finite; a program needn't handle non-finite values.
Results may differ from a plain program's by a relative error of at most 0.0016.
The roundings to bfloat16 on the way count: a program that leaves them out, or rounds other values in their place, can miss the bound.
Values may be sent and summed in bfloat16 or wider, within the bound.
A program may use at most 64 MiB of HBM per device.

v0:
```python
import math

import jax
import jax.numpy as jnp
from jax import lax
from jax.sharding import PartitionSpec as P

NF = 36
ND = 36
TS = 8
NSUB = 2
K = 1296
PCAP = 256


GRAVITY = 9.81
FREQ_BASE = 0.035
FREQ_RATIO = 1.1
TIME_STEP = 450.0
CELL_SIZE = 27750.0
LAT_EDGE = 64.0 * math.pi / 180.0
WIND_RATE = 0.1
BREAK_RATE = 0.15
ENERGY_REF = 1.5
TRANSFER_RATE = 0.2
KH_LIMIT = 10.0


def padded(value, sides, width):
    for axis, dim in sides:
        devices, length = (lax.axis_size(axis), value.shape[dim])
        up = [(i, (i + 1) % devices) for i in range(devices)]
        down = [(j, i) for i, j in up]
        last = lax.slice_in_dim(value, length - width, length, axis=dim)
        leading = lax.slice_in_dim(value, 0, width, axis=dim)
        before = lax.ppermute(last, axis, up)
        after = lax.ppermute(leading, axis, down)
        value = jnp.concatenate([before, value, after], axis=dim)
    return value


def frequencies(how_many):
    return FREQ_BASE * jnp.power(jnp.float32(FREQ_RATIO), jnp.arange(how_many).astype(jnp.float32))


def directions(how_many):
    return 2.0 * math.pi * (jnp.arange(how_many).astype(jnp.float32) + 0.5) / how_many


def row_metric(rows_total):
    latitude = LAT_EDGE * (
        2.0 * (jnp.arange(rows_total).astype(jnp.float32) + 0.5) / rows_total - 1.0
    )
    return jnp.cos(latitude)


def group_speed(frequency, sea_depth):
    angular = 2.0 * math.pi * frequency
    deep_number = angular * angular / GRAVITY
    wavenumber = deep_number / jnp.sqrt(jnp.tanh(deep_number * sea_depth))
    relative = jnp.minimum(wavenumber * sea_depth, KH_LIMIT)
    group_ratio = 0.5 + relative / jnp.sinh(2.0 * relative)
    return group_ratio * angular / wavenumber


def source_terms(spectrum_block, wind_speed, heading, freq_kernel, dir_kernel):
    freq_count = freq_kernel.shape[0]
    dir_count = dir_kernel.shape[0]
    points = spectrum_block.shape[1]
    energy = spectrum_block.astype(jnp.float32).reshape(freq_count, dir_count, points)
    frequency = frequencies(freq_count)
    angles = directions(dir_count)
    weighted = jnp.sum(energy, axis=1) * frequency[:, None]
    first_moment = jnp.sum(weighted, axis=0)
    mean_energy = first_moment / (dir_count * jnp.sum(frequency))
    mean_freq = jnp.sum(weighted * frequency[:, None], axis=0) / first_moment
    phase_speed = GRAVITY / (2.0 * math.pi * frequency)
    forcing = (
        wind_speed[None, None, :]
        / phase_speed[:, None, None]
        * jnp.cos(angles[None, :, None] - heading[None, None, :])
        - 1.0
    )
    growth = WIND_RATE * jnp.maximum(forcing, 0.0)
    damping = (
        BREAK_RATE
        * (frequency[:, None, None] / mean_freq[None, None, :])
        * jnp.square(mean_energy / ENERGY_REF)[None, None, :]
    )
    coupled = jnp.einsum("ab,bjp->ajp", freq_kernel, energy, precision=lax.Precision.HIGHEST)
    coupled = jnp.einsum("cj,ajp->acp", dir_kernel, coupled, precision=lax.Precision.HIGHEST)
    transfer = TRANSFER_RATE * energy * coupled / mean_energy[None, None, :]
    updated = (energy + growth * energy + transfer) / (1.0 + damping)
    return updated.reshape(freq_count * dir_count, points).astype(jnp.bfloat16)


def window(values, begin_at, end_at, along):
    return lax.slice_in_dim(values, begin_at, end_at, axis=along)


def upwind_sweep(density, courant, sea_mask, along):
    length = density.shape[along]
    behind = window(density, 0, length - 3, along)
    centre = window(density, 1, length - 2, along)
    ahead_one = window(density, 2, length - 1, along)
    beyond = window(density, 3, length, along)
    face_courant = 0.5 * (
        window(courant, 1, length - 2, along) + window(courant, 2, length - 1, along)
    )
    face_courant = (
        face_courant
        * window(sea_mask, 1, length - 2, along)
        * window(sea_mask, 2, length - 1, along)
    )
    curvature = (1.0 - face_courant * face_courant) / 6.0
    middle = 0.5 * (centre + ahead_one) - 0.5 * face_courant * (ahead_one - centre)
    upstream = jnp.where(
        face_courant > 0.0, ahead_one - 2.0 * centre + behind, beyond - 2.0 * ahead_one + centre
    )
    face_flux = face_courant * (middle - curvature * upstream)
    return window(density, 2, length - 2, along) - (
        window(face_flux, 1, length - 3, along) - window(face_flux, 0, length - 4, along)
    )


def column_sweep(density, courant, sea_mask):
    widths = ((0, 0), (0, 0), (2, 2))
    return upwind_sweep(
        jnp.pad(density, widths), jnp.pad(courant, widths), jnp.pad(sea_mask, widths), 2
    )


def layout_maps(mask_strip, owners, owner_count):
    strip_width, strip_height = mask_strip.shape
    tiles_across = strip_width // TS
    tiles_down = strip_height // TS
    tile_cells = (
        mask_strip.reshape(tiles_across, TS, tiles_down, TS)
        .transpose(0, 2, 1, 3)
        .reshape(tiles_across * tiles_down, TS * TS)
    )
    counts = jnp.sum(tile_cells, axis=1)
    tile_index = jnp.arange(tiles_across * tiles_down)
    earlier = (owners[None, :] == owners[:, None]) & (tile_index[None, :] < tile_index[:, None])
    offsets = jnp.sum(jnp.where(earlier, counts[None, :], 0), axis=1)
    rank_within = jnp.cumsum(tile_cells, axis=1) - tile_cells
    columns = owners[:, None] * PCAP + offsets[:, None] + rank_within
    columns = (
        columns.reshape(tiles_across, tiles_down, TS, TS)
        .transpose(0, 2, 1, 3)
        .reshape(strip_width * strip_height)
    )
    sea_cells = mask_strip.reshape(strip_width * strip_height)
    targets = jnp.where(sea_cells == 1, columns, owner_count * PCAP)
    cell_numbers = jnp.arange(strip_width * strip_height)
    slot_cell = (
        jnp.zeros((owner_count * PCAP,), jnp.int32).at[targets].set(cell_numbers, mode="drop")
    )
    filled = (
        jnp.zeros((owner_count * PCAP,), jnp.int32)
        .at[targets]
        .set(jnp.ones_like(cell_numbers), mode="drop")
    )
    return (columns, sea_cells, slot_cell, filled)


def local(
    spectrum, wind_speed, wind_dir, freq_kernel, dir_kernel, depth, current, land_mask, tile_owner
):
    owner_count = lax.axis_size("comp") * lax.axis_size("sub")
    group_size = -(-K // owner_count)
    padded_count = group_size * owner_count
    strip_width, strip_height = land_mask.shape
    columns, sea_cells, slot_cell, filled = layout_maps(land_mask, tile_owner[0], owner_count)
    rim_width = 2
    cell_stack = jnp.stack([depth, current[0], current[1], land_mask.astype(jnp.float32)])
    fields = padded(cell_stack.astype(jnp.bfloat16), (("tile", 1),), rim_width).astype(
        cell_stack.dtype
    )
    source = source_terms(spectrum[0, 0], wind_speed[0, 0], wind_dir[0, 0], freq_kernel, dir_kernel)
    outgoing = jnp.pad(source, ((0, padded_count - K), (0, 0)))
    arrived = lax.all_to_all(outgoing, ("comp", "sub"), split_axis=0, concat_axis=1, tiled=True)
    gathered = jnp.take(arrived, columns, axis=1, mode="clip")
    density = jnp.where(sea_cells[None, :] == 1, gathered.astype(jnp.float32), 0.0).reshape(
        group_size, strip_width, strip_height
    )
    group_index = lax.axis_index("comp") * lax.axis_size("sub") + lax.axis_index("sub")
    component = group_index * group_size + jnp.arange(group_size)
    frequency = frequencies(NF)[jnp.minimum(component // ND, NF - 1)]
    comp_angle = directions(ND)[component % ND]
    metric = row_metric(strip_height)
    group_vel = group_speed(frequency[:, None, None], fields[0][None])
    along_x = (
        (group_vel * jnp.cos(comp_angle)[:, None, None] + fields[1][None])
        * TIME_STEP
        / (CELL_SIZE * metric[None, None, :])
    )
    along_y = (
        (group_vel * jnp.sin(comp_angle)[:, None, None] + fields[2][None]) * TIME_STEP / CELL_SIZE
    )
    sea_field = fields[3][None]
    total_width = strip_width + 2 * rim_width
    inner_y = window(along_y, 2, total_width - 2, 1)
    inner_sea = window(sea_field, 2, total_width - 2, 1)
    for substep in range(NSUB):
        extended = padded(density, (("tile", 1),), 2)
        density = upwind_sweep(extended, along_x, sea_field, 1)
        density = column_sweep(density, inner_y, inner_sea)
    leaving = density.astype(jnp.bfloat16).reshape(group_size, strip_width * strip_height)
    picked = jnp.take(leaving, slot_cell, axis=1, mode="clip")
    picked = jnp.where(filled[None, :] == 1, picked, jnp.zeros((), jnp.bfloat16))
    returned = lax.all_to_all(picked, ("comp", "sub"), split_axis=1, concat_axis=0, tiled=True)
    return returned[:K].reshape(1, 1, K, PCAP)


def solution(mesh):
    placed = (
        P(("ens", "tile"), ("comp", "sub"), None, None),
        P(("ens", "tile"), ("comp", "sub"), None),
        P(("ens", "tile"), ("comp", "sub"), None),
        P(),
        P(),
        P("tile", None),
        P(None, "tile", None),
        P("tile", None),
        P("tile", None),
    )
    return jax.shard_map(
        local,
        mesh=mesh,
        in_specs=placed,
        out_specs=P(("ens", "tile"), ("comp", "sub"), None, None),
        check_vma=False,
    )
```

profile of v0, /device:TPU:0, one launch (start us, length us, event | category | flops | bytes accessed | tf_op | source)
XLA Modules:
  0.0 130.3 jit_solution(10856687681883370346)
XLA Ops:
  0.0 0.7 convert_bitcast_fusion
  0.7 0.7 fusion.50
  1.4 0.7 convert.13
  2.1 3.0 %collective-permute-start = (bf16[4,2,128]{2,1,0:T(2,128)(2,1)S(1)}, bf16[4,2,128]{2,1,0:T(2,128)(2,1)S(1)}, u32[]{:S(2)}, u32[]{:S(2)}) collective-permute-start(bf16[4,2,128]{2,1,0:T(2,128)(2,1)S(1)} %get-tuple-element.18), channel_id=1, source_target_pairs={{0,2},{2,0},{1,3},{3,1},{4,6},{6,4},{5,7},{7,5},{8,10},{10,8},{9,1... | collective-permute-start | bytes 6152 | tf_op jit(solution)/shard_map/ppermute | solution.py:36
  5.1 0.1 collective-permute-start.1
  5.2 0.6 fusion.57
  5.9 1.2 squeeze.3
  7.1 0.2 convert_reduce_fusion
  7.3 0.7 fusion.40
  8.7 0.1 broadcast_divide_fusion
  8.8 0.1 multiply_reduce_fusion
  8.9 0.2 fusion.42
  9.1 2.5 %fusion.37 = bf16[36,36,256]{2,1,0:T(8,128)(2,1)S(1)} fusion(bf16[36,36,256]{2,1,0:T(8,128)(2,1)S(1)} %squeeze.3, f32[36,36,256]{2,0,1:T(8,128)S(1)} %fusion.40, f32[36,256]{1,0:T(8,128)S(1)} %get-tuple-element.31, f32[256]{0:T(256)S(1)} %get-tuple-element.8, f32[36,256]{1,0:T(8,128)S(1)} %get-tuple-element.32, f32[36,256]{1,0:T(8,128)S(1)} %broadcast_divide_fusion, ...), kind=kOutput, calls=%fused_computation.75 | convolution fusion | flops 147640320 | bytes 2771008 | tf_op jit(solution)/shard_map/cj,ajp->acp/dot_general | solution.py:91
  11.7 1.0 convert_element_type.85
  12.7 5.3 %all-to-all-start = ((bf16[8,162,256]{2,1,0:T(8,128)(2,1)}), bf16[8,162,256]{2,1,0:T(8,128)(2,1)S(1)}, u32[]{:S(2)}, u32[]{:S(2)}) async-start(bf16[8,162,256]{2,1,0:T(8,128)(2,1)} %convert_element_type.85), calls=%async_computation | async-start | bytes 1376256 | tf_op jit(solution)/shard_map/all_to_all | solution.py:182
  18.1 0.1 reshape.352
  18.2 0.1 mul.379
  18.3 0.1 bitcast_reduce_fusion
  18.4 0.1 broadcast_in_dim.70
  18.5 0.2 select_reduce_fusion
  18.7 0.1 reduce_sum.58
  18.8 0.1 copy.19
  18.9 0.1 reshape.353
  19.0 0.1 copy.20
  19.0 0.2 reduce_window_sum.13
  19.3 0.1 copy.21
  19.4 0.1 reduce_window_sum.14
  19.5 0.1 copy.22
  19.6 0.1 add_bitcast_fusion
  19.7 0.1 reshape.360
  19.8 0.1 reshape.354
  20.0 1.6 %gather_fusion.1 = f32[162]{0:T(256)S(1)} fusion(f32[36]{0:T(128)S(1)} %fusion.56, s32[1024]{0:T(1024)S(1)} %pad_clamp_fusion.1), kind=kCustom, calls=%fused_computation.1 | custom fusion | bytes 1944 | tf_op jit(solution)/shard_map/gather | solution.py:189
  21.5 1.6 %gather_fusion.2 = f32[162]{0:T(256)S(1)} fusion(f32[36]{0:T(128)S(1)} %add_multiply_fusion, s32[1024]{0:T(1024)S(1)} %pad_clamp_fusion), kind=kCustom, calls=%fused_computation.2 | custom fusion | bytes 1944 | tf_op jit(solution)/shard_map/gather | solution.py:190
  23.2 8.0 %scatter_custom_fusion = s32[2048]{0:T(1024)S(1)} fusion(s32[2048]{0:T(1024)S(1)} %bitcast.77, s32[2048]{0:T(1024)S(1)} %broadcast.431, s32[]{:T(128)} %constant.38.clone.1), kind=kCustom, calls=%fused_computation.121 | custom fusion | bytes 8196 | tf_op jit(solution)/shard_map/scatter | solution.py:162
  31.3 8.2 %scatter_custom_fusion.1 = s32[2048]{0:T(1024)S(1)} fusion(s32[2048]{0:T(1024)S(1)} %bitcast.78, s32[2048]{0:T(1024)S(1)} %iota.51, s32[]{:T(128)} %constant.38.clone.1), kind=kCustom, calls=%fused_computation.119 | custom fusion | bytes 8196 | tf_op jit(solution)/shard_map/scatter | solution.py:157
  39.6 3.8 %multiply_divide_fusion.1 = (f32[162,20,128]{0,2,1:T(8,128)S(1)}, f32[162,20,128]{0,2,1:T(8,128)S(1)}) fusion(f32[162]{0:T(256)S(1)} %get-tuple-element.27, f32[20,128]{1,0:T(8,128)S(1)} %get-tuple-element.15, f32[162]{0:T(256)S(1)} %get-tuple-element.26, f32[128]{0:T(128)S(1)} %cosine_multiply_fusion, f32[20,128]{1,0:T(8,128)S(1)} %get-tuple-element.14, ...), kind=kLoop, calls=%fused_computation.11 | loop fusion | flops 9538560 | bytes 3340696 | tf_op jit(solution)/shard_map/div | solution.py:63
  43.5 1.7 %fusion.29 = f32[162,16,128]{0,2,1:T(8,128)} fusion(f32[162,20,128]{0,2,1:T(8,128)S(1)} %get-tuple-element.20, f32[16,128]{1,0:T(8,128)S(1)} %slice.221, f32[162]{0:T(256)S(1)} %get-tuple-element.24), kind=kLoop, calls=%fused_computation.66 | loop fusion | flops 995328 | bytes 2663048 | tf_op jit(solution)/shard_map/div | solution.py:199
  45.2 1.3 copy.25
  46.5 9.8 %gather_fusion = bf16[2048,162]{1,0:T(8,128)(2,1)} fusion(bf16[162,2048]{0,1:T(8,128)(2,1)} %bitcast.70, s32[2048]{0:T(1024)S(1)} %broadcast_clamp_fusion.1), kind=kCustom, calls=%fused_computation | custom fusion | bytes 1335296 | tf_op jit(solution)/shard_map/jit(_take)/gather | solution.py:183
  56.3 1.4 %convert_element_type.93 = f32[2048,162]{1,0:T(8,128)S(1)} convert(bf16[2048,162]{1,0:T(8,128)(2,1)} %gather_fusion) | non-fusion elementwise | flops 331776 | bytes 1990656 | tf_op jit(solution)/shard_map/convert_element_type | solution.py:184
  57.7 0.3 broadcast_select_fusion
  58.1 1.6 %collective-permute-start.2 = (f32[162,2,128]{0,2,1:T(8,128)S(1)}, f32[162,2,128]{0,2,1:T(8,128)S(1)}, u32[]{:S(2)}, u32[]{:S(2)}) collective-permute-start(f32[162,2,128]{0,2,1:T(8,128)S(1)} %get-tuple-element.11), channel_id=1, source_target_pairs={{0,2},{2,0},{1,3},{3,1},{4,6},{6,4},{5,7},{7,5},{8,10},{10,8},{9,1... | collective-permute-start | bytes 497672 | tf_op jit(solution)/shard_map/ppermute | solution.py:36
  59.6 0.5 collective-permute-start.3
  60.2 0.1 fusion.46
  60.3 7.0 %collective-permute-done.2 = f32[162,2,128]{0,2,1:T(8,128)S(1)} collective-permute-done((f32[162,2,128]{0,2,1:T(8,128)S(1)}, f32[162,2,128]{0,2,1:T(8,128)S(1)}, u32[]{:S(2)}, u32[]{:S(2)}) %collective-permute-start.2) | collective-permute-done | bytes 165920 | tf_op jit(solution)/shard_map/ppermute | solution.py:36
  67.3 5.2 %collective-permute-done.3 = f32[162,2,128]{0,2,1:T(8,128)S(1)} collective-permute-done((f32[162,2,128]{0,2,1:T(8,128)S(1)}, f32[162,2,128]{0,2,1:T(8,128)S(1)}, u32[]{:S(2)}, u32[]{:S(2)}) %collective-permute-start.3) | collective-permute-done | bytes 165920 | tf_op jit(solution)/shard_map/ppermute | solution.py:37
  72.5 2.1 %fusion.20 = f32[162,17,128]{0,2,1:T(8,128)S(1)} fusion(f32[162,2,128]{0,2,1:T(8,128)S(1)} %collective-permute-done.3, f32[162,16,128]{0,2,1:T(8,128)S(1)} %broadcast_select_fusion, f32[162,2,128]{0,2,1:T(8,128)S(1)} %collective-permute-done.2, f32[17,128]{1,0:T(8,128)S(1)} %get-tuple-element.17, f32[17,128]{1,0:T(8,128)S(1)} %get-tuple-element.16, ...), kind=kLoop, calls=%fused_computation.46 | loop fusion | flops 9517824 | bytes 5906432 | tf_op jit(solution)/shard_map/mul | solution.py:120
  74.6 0.5 fusion.30
  75.1 1.1 copy-done.1
  76.2 2.6 %subtract_multiply_fusion.1 = f32[162,16,129]{0,2,1:T(8,128)S(1)} fusion(f32[162,16,128]{0,2,1:T(8,128)S(1)} %fusion.30, f32[16,129]{1,0:T(8,128)S(1)} %get-tuple-element.23, f32[16,129]{1,0:T(8,128)S(1)} %get-tuple-element.22, f32[162,16,128]{0,2,1:T(8,128)S(1)} %copy-done.1), kind=kLoop, calls=%fused_computation.53 | loop fusion | flops 7690464 | bytes 4008192 | tf_op jit(solution)/shard_map/mul | solution.py:120
  78.7 0.3 fusion.27
  79.1 1.6 %collective-permute-start.4 = (f32[162,2,128]{0,2,1:T(8,128)S(1)}, f32[162,2,128]{0,2,1:T(8,128)S(1)}, u32[]{:S(2)}, u32[]{:S(2)}) collective-permute-start(f32[162,2,128]{0,2,1:T(8,128)S(1)} %get-tuple-element.9), channel_id=1, source_target_pairs={{0,2},{2,0},{1,3},{3,1},{4,6},{6,4},{5,7},{7,5},{8,10},{10,8},{9,1... | collective-permute-start | bytes 497672 | tf_op jit(solution)/shard_map/ppermute | solution.py:36
  80.6 0.5 collective-permute-start.5
  81.2 7.2 %collective-permute-done.4 = f32[162,2,128]{0,2,1:T(8,128)S(1)} collective-permute-done((f32[162,2,128]{0,2,1:T(8,128)S(1)}, f32[162,2,128]{0,2,1:T(8,128)S(1)}, u32[]{:S(2)}, u32[]{:S(2)}) %collective-permute-start.4) | collective-permute-done | bytes 165920 | tf_op jit(solution)/shard_map/ppermute | solution.py:36
  88.4 4.3 %collective-permute-done.5 = f32[162,2,128]{0,2,1:T(8,128)S(1)} collective-permute-done((f32[162,2,128]{0,2,1:T(8,128)S(1)}, f32[162,2,128]{0,2,1:T(8,128)S(1)}, u32[]{:S(2)}, u32[]{:S(2)}) %collective-permute-start.5) | collective-permute-done | bytes 165920 | tf_op jit(solution)/shard_map/ppermute | solution.py:37
  92.7 2.1 %fusion.13 = f32[162,17,128]{0,2,1:T(8,128)S(1)} fusion(f32[162,2,128]{0,2,1:T(8,128)S(1)} %collective-permute-done.5, f32[162,16,128]{0,2,1:T(8,128)S(1)} %fusion.27, f32[162,2,128]{0,2,1:T(8,128)S(1)} %collective-permute-done.4, f32[17,128]{1,0:T(8,128)S(1)} %get-tuple-element.17, f32[17,128]{1,0:T(8,128)S(1)} %get-tuple-element.16, ...), kind=kLoop, calls=%fused_computation.37 | loop fusion | flops 9517824 | bytes 5906432 | tf_op jit(solution)/shard_map/mul | solution.py:120
  94.8 0.3 fusion.26
  95.1 2.6 %subtract_multiply_fusion = f32[162,16,129]{0,2,1:T(8,128)S(1)} fusion(f32[162,16,128]{0,2,1:T(8,128)S(1)} %fusion.26, f32[16,129]{1,0:T(8,128)S(1)} %get-tuple-element.23, f32[16,129]{1,0:T(8,128)S(1)} %get-tuple-element.22, f32[162,16,128]{0,2,1:T(8,128)S(1)} %copy-done.1), kind=kLoop, calls=%fused_computation.52 | loop fusion | flops 7690464 | bytes 4008192 | tf_op jit(solution)/shard_map/mul | solution.py:120
  97.7 0.5 fusion.25
  98.1 7.5 %gather_fusion.3 = bf16[2048,162]{1,0:T(8,128)(2,1)S(1)} fusion(bf16[162,2048]{0,1:T(8,128)(2,1)S(1)} %bitcast.69, s32[2048]{0:T(1024)S(1)} %broadcast_clamp_fusion), kind=kCustom, calls=%fused_computation.3 | custom fusion | bytes 1335296 | tf_op jit(solution)/shard_map/jit(_take)/gather | solution.py:210
  105.6 0.5 copy.26
  106.2 0.1 broadcast_select_fusion.1
  106.2 23.0 %all_to_all.29 = bf16[162,8,256]{2,0,1:T(8,128)(2,1)S(1)} all-to-all(bf16[162,8,256]{2,0,1:T(8,128)(2,1)S(1)} %broadcast_select_fusion.1), channel_id=1, replica_groups=mesh['ens'=2,'comp'=4,'tile'=2,'sub'=2] {'comp','sub'}, dimensions={1} | all-to-all | bytes 1327104 | tf_op jit(solution)/shard_map/all_to_all | solution.py:212
  129.3 1.0 reshape.356
  (45 shorter events, 0.4 us)
Async XLA Ops:
  0.0 7.3 %copy-start = (f32[36,36]{1,0:T(8,128)S(1)}, f32[36,36]{1,0:T(8,128)}, u32[]{:S(2)}) copy-start(f32[36,36]{1,0:T(8,128)} %param.12) | copy-start | bytes 15556
  2.1 6.6 %copy-start.5 = (f32[1,1,256]{2,1,0:T(1,128)S(1)}, f32[1,1,256]{2,1,0:T(1,128)}, u32[]{:S(2)}) copy-start(f32[1,1,256]{2,1,0:T(1,128)} %param.10) | copy-start | bytes 3076
  2.1 37.4 %collective-permute-start = (bf16[4,2,128]{2,1,0:T(2,128)(2,1)S(1)}, bf16[4,2,128]{2,1,0:T(2,128)(2,1)S(1)}, u32[]{:S(2)}, u32[]{:S(2)}) collective-permute-start(bf16[4,2,128]{2,1,0:T(2,128)(2,1)S(1)} %get-tuple-element.18), channel_id=1, source_target_pairs={{0,2},{2,0},{1,3},{3,1},{4,6},{6,4},{5,7},{7,5},{8,10},{10,8},{9,1... | collective-permute-start | bytes 6152 | tf_op jit(solution)/shard_map/ppermute | solution.py:36
  5.1 34.4 %collective-permute-start.1 = (bf16[4,2,128]{2,1,0:T(2,128)(2,1)S(1)}, bf16[4,2,128]{2,1,0:T(2,128)(2,1)S(1)}, u32[]{:S(2)}, u32[]{:S(2)}) collective-permute-start(bf16[4,2,128]{2,1,0:T(2,128)(2,1)S(1)} %get-tuple-element.19), channel_id=1, source_target_pairs={{2,0},{0,2},{3,1},{1,3},{6,4},{4,6},{7,5},{5,7},{10,8},{8,10},{11,... | collective-permute-start | bytes 6152 | tf_op jit(solution)/shard_map/ppermute | solution.py:37
  5.9 3.0 %copy-start.4 = (f32[1,1,256]{2,1,0:T(1,128)S(1)}, f32[1,1,256]{2,1,0:T(1,128)}, u32[]{:S(2)}) copy-start(f32[1,1,256]{2,1,0:T(1,128)} %param.11) | copy-start | bytes 3076
  5.9 3.3 %copy-start.6 = (f32[36,36]{1,0:T(8,128)S(1)}, f32[36,36]{1,0:T(8,128)}, u32[]{:S(2)}) copy-start(f32[36,36]{1,0:T(8,128)} %param.13) | copy-start | bytes 15556
  11.6 6.4 %copy-start.2 = (s32[16,128]{1,0:T(8,128)S(1)}, s32[16,128]{1,0:T(8,128)}, u32[]{:S(2)}) copy-start(s32[16,128]{1,0:T(8,128)} %param.16) | copy-start | bytes 24580
  11.7 6.5 %copy-start.3 = (s32[1,32]{1,0:T(1,128)S(1)}, s32[1,32]{1,0:T(1,128)}, u32[]{:S(2)}) copy-start(s32[1,32]{1,0:T(1,128)} %param.17) | copy-start | bytes 388
  12.7 32.5 %all-to-all-start = ((bf16[8,162,256]{2,1,0:T(8,128)(2,1)}), bf16[8,162,256]{2,1,0:T(8,128)(2,1)S(1)}, u32[]{:S(2)}, u32[]{:S(2)}) async-start(bf16[8,162,256]{2,1,0:T(8,128)(2,1)} %convert_element_type.85), calls=%async_computation | async-start | bytes 1376256 | tf_op jit(solution)/shard_map/all_to_all | solution.py:182
  58.1 9.2 %collective-permute-start.2 = (f32[162,2,128]{0,2,1:T(8,128)S(1)}, f32[162,2,128]{0,2,1:T(8,128)S(1)}, u32[]{:S(2)}, u32[]{:S(2)}) collective-permute-start(f32[162,2,128]{0,2,1:T(8,128)S(1)} %get-tuple-element.11), channel_id=1, source_target_pairs={{0,2},{2,0},{1,3},{3,1},{4,6},{6,4},{5,7},{7,5},{8,10},{10,8},{9,1... | collective-permute-start | bytes 497672 | tf_op jit(solution)/shard_map/ppermute | solution.py:36
  59.6 12.8 %collective-permute-start.3 = (f32[162,2,128]{0,2,1:T(8,128)S(1)}, f32[162,2,128]{0,2,1:T(8,128)S(1)}, u32[]{:S(2)}, u32[]{:S(2)}) collective-permute-start(f32[162,2,128]{0,2,1:T(8,128)S(1)} %get-tuple-element.12), channel_id=1, source_target_pairs={{2,0},{0,2},{3,1},{1,3},{6,4},{4,6},{7,5},{5,7},{10,8},{8,10},{11,... | collective-permute-start | bytes 497672 | tf_op jit(solution)/shard_map/ppermute | solution.py:37
  74.6 1.6 %copy-start.1 = (f32[162,16,128]{0,2,1:T(8,128)S(1)}, f32[162,16,128]{0,2,1:T(8,128)}, u32[]{:S(2)}) copy-start(f32[162,16,128]{0,2,1:T(8,128)} %fusion.29) | copy-start | bytes 3981316
  79.1 9.3 %collective-permute-start.4 = (f32[162,2,128]{0,2,1:T(8,128)S(1)}, f32[162,2,128]{0,2,1:T(8,128)S(1)}, u32[]{:S(2)}, u32[]{:S(2)}) collective-permute-start(f32[162,2,128]{0,2,1:T(8,128)S(1)} %get-tuple-element.9), channel_id=1, source_target_pairs={{0,2},{2,0},{1,3},{3,1},{4,6},{6,4},{5,7},{7,5},{8,10},{10,8},{9,1... | collective-permute-start | bytes 497672 | tf_op jit(solution)/shard_map/ppermute | solution.py:36
  80.6 12.0 %collective-permute-start.5 = (f32[162,2,128]{0,2,1:T(8,128)S(1)}, f32[162,2,128]{0,2,1:T(8,128)S(1)}, u32[]{:S(2)}, u32[]{:S(2)}) collective-permute-start(f32[162,2,128]{0,2,1:T(8,128)S(1)} %get-tuple-element.10), channel_id=1, source_target_pairs={{2,0},{0,2},{3,1},{1,3},{6,4},{4,6},{7,5},{5,7},{10,8},{8,10},{11,... | collective-permute-start | bytes 497672 | tf_op jit(solution)/shard_map/ppermute | solution.py:37
where the time goes:
time: 131 us; the launch traced here: 130 us
  local copies, waits for them, and re-layouts  44.2 us (34%)
  waiting for transfers between devices  23.7 us (18%)
  blocking collectives  23 us (18%)
  other arithmetic  22.3 us (17%)
  starting transfers between devices  12.6 us (10%)
  matrix products  3.24 us (2%)
    all_to_all x1, blocking collectives, local(): lax.all_to_all(picked, ('comp', 'sub'), split_axis=1, concat_axis=0, tile...  23 us
    ppermute x3, waiting for transfers between devices, padded(): before = lax.ppermute(last, axis, up)  14.2 us
    gather x1, local copies, waits for them, and re-layouts, local(): gathered = jnp.take(arrived, columns, axis=1, mode='clip')  9.83 us
    ppermute x3, waiting for transfers between devices, padded(): after = lax.ppermute(leading, axis, down)  9.56 us
    mul x4, other arithmetic, upwind_sweep(): face_flux = face_courant * (middle - curvature * upstream)  9.32 us
    scatter x1, local copies, waits for them, and re-layouts, layout_maps(): jnp.zeros((owner_count * PCAP,), jnp.int32).at[targets]  8.23 us
    scatter x1, local copies, waits for them, and re-layouts, layout_maps(): filled = jnp.zeros((owner_count * PCAP,), jnp.int32).at[targets].set(jnp....  8.05 us
    gather x2, local copies, waits for them, and re-layouts, local(): picked = jnp.take(leaving, slot_cell, axis=1, mode='clip')  8.02 us
  transfers between devices with their start and end apart: 7, of which 4 were waited for; matrix products, arithmetic and copies ran while one was open for 26% of the time, Pallas kernels for 0%

commit v1 on v0

--- a/solution.py
+++ b/solution.py
@@ -3,6 +3,8 @@
 import jax
 import jax.numpy as jnp
 from jax import lax
+from jax.experimental import pallas as pl
+from jax.experimental.pallas import tpu as pltpu
 from jax.sharding import PartitionSpec as P
 
 NF = 36
@@ -213,7 +215,387 @@
     return returned[:K].reshape(1, 1, K, PCAP)
 
 
+OWNERS = 8
+STRIPS = 2
+GROUP = OWNERS * STRIPS
+RANKS = 4
+ROWS = 80
+EXTRA = 16
+CAP = ROWS + EXTRA
+LAST = GROUP - 1
+PARTS = ((0, 48), (48, 32))
+PART_ROWS = 48
+WIDE = 32
+TALL = 128
+FIELD_ROWS = 72
+
+
+def butterfly(values, pieces):
+    for bit in range(3):
+        step = 1 << bit
+        odd = (pieces & step) != 0
+        values = [jnp.where(odd, values[(j + step) % 8], values[j]) for j in range(8)]
+    return values
+
+
+def turn(values, by):
+    by %= values.shape[0]
+    if by == 0:
+        return values
+    return jnp.concatenate([values[-by:], values[:-by]], axis=0)
+
+
+def first_sweep(d, face, bend):
+    ahead = turn(d, -1)
+    slope = ahead - d
+    second = slope - turn(slope, 1)
+    upstream = jnp.where(face > 0.0, second, turn(second, -1))
+    flux = face * (0.5 * (d + ahead) - 0.5 * face * slope - bend * upstream)
+    return d - (flux - turn(flux, 1))
+
+
+def second_sweep(d, face, bend, lane):
+    shape = d.shape
+    flat = lambda v: v.reshape(shape[0] * shape[1], shape[2])
+    d, face, bend = flat(d), flat(face), flat(bend)
+    ahead = jnp.where(lane == TALL - 1, 0.0, pltpu.roll(d, TALL - 1, 1))
+    slope = ahead - d
+    second = slope - jnp.where(lane == 0, d, pltpu.roll(slope, 1, 1))
+    upstream = jnp.where(face > 0.0, second, pltpu.roll(second, TALL - 1, 1))
+    flux = face * (0.5 * (d + ahead) - 0.5 * face * slope - bend * upstream)
+    return (d - (flux - pltpu.roll(flux, 1, 1))).reshape(shape)
+
+
+def exchange_kernel(
+    source_ref, place_ref, field_ref, small_ref, angle_ref, out_ref,
+    packed, arrived, fields, density, leaving, first_rate, second_rate, drift, tile_map,
+    go_send, go_recv, go_extra_send, go_extra_recv,
+    back_send, back_recv, back_extra_send, back_extra_recv, field_send, field_recv,
+):
+    comp, tile, sub = lax.axis_index("comp"), lax.axis_index("tile"), lax.axis_index("sub")
+    me = tile * OWNERS + comp * 2 + sub
+
+    def partner(dc, dt, ds):
+        c, t, s = lax.rem(comp + dc, 4), lax.rem(tile + dt, 2), lax.rem(sub + ds, 2)
+        return t * OWNERS + c * 2 + s, {"comp": c, "tile": t, "sub": s}
+
+    turns = [(dc, dt, ds) for dc in (2, 1, 3, 0) for dt in (0, 1) for ds in (0, 1)]
+    turns = [item for item in turns if item != (0, 0, 0)]
+    partners = [partner(*item) for item in turns]
+    final_device = {"comp": 3, "tile": 1, "sub": 1}
+
+    barrier = pltpu.get_barrier_semaphore()
+    for _, where in partners:
+        pl.semaphore_signal(barrier, inc=1, device_id=where, device_id_type=pl.DeviceIdType.MESH)
+    pl.semaphore_wait(barrier, GROUP - 1)
+
+    def remote(src, dst, send, recv, where):
+        return pltpu.make_async_remote_copy(
+            src_ref=src, dst_ref=dst, send_sem=send, recv_sem=recv,
+            device_id=where, device_id_type=pl.DeviceIdType.MESH,
+        )
+
+    beside = partner(0, 1, 0)[1]
+    field_copy = remote(field_ref, fields.at[tile], field_send, field_recv, beside)
+    field_copy.start()
+
+    packed[...] = jnp.dot(
+        source_ref[...], place_ref[...], preferred_element_type=jnp.float32
+    ).astype(jnp.bfloat16)
+
+    def aligned(value):
+        return pl.multiple_of(value, 16)
+
+    def go(part, number, where):
+        at, rows = PARTS[part]
+        return remote(
+            packed.at[pl.ds(aligned(number * ROWS + at), rows)],
+            arrived.at[me, pl.ds(at, rows)],
+            go_send.at[part, number], go_recv.at[part, me], where,
+        )
+
+    def go_landed(part, number, where):
+        at, rows = PARTS[part]
+        spot = arrived.at[number, pl.ds(at, rows)]
+        return remote(spot, spot, go_send.at[part, number], go_recv.at[part, number], where)
+
+    def go_extra():
+        return remote(
+            packed.at[pl.ds(GROUP * ROWS, EXTRA)], arrived.at[me, pl.ds(ROWS, EXTRA)],
+            go_extra_send, go_extra_recv.at[me], final_device,
+        )
+
+    for part in range(len(PARTS)):
+        for number, where in partners:
+            go(part, number, where).start()
+
+    @pl.when(me != LAST)
+    def _():
+        go_extra().start()
+
+    arrived[me, pl.ds(0, ROWS)] = packed[pl.ds(aligned(me * ROWS), ROWS), :]
+
+    @pl.when(me == LAST)
+    def _():
+        arrived[LAST, pl.ds(ROWS, EXTRA)] = packed[pl.ds(GROUP * ROWS, EXTRA), :]
+
+    @pl.when(me != LAST)
+    def _():
+        for number in range(GROUP):
+            arrived[number, pl.ds(ROWS, EXTRA)] = jnp.zeros((EXTRA, 256), jnp.bfloat16)
+
+    fields[tile] = field_ref[...]
+    field_copy.wait()
+
+    lane = lax.broadcasted_iota(jnp.int32, (1, TALL), 1)
+    row_number = lax.broadcasted_iota(jnp.int32, (256, TALL), 0)
+    for strip in range(STRIPS):
+        for half in range(2):
+            target = fields[strip, pl.ds(64 + half, 1), :].astype(jnp.int32)
+            tile_map[strip, :, pl.ds(half * TALL, TALL)] = jnp.where(
+                row_number == target, 1.0, 0.0
+            ).astype(jnp.bfloat16)
+
+    def whole(at):
+        return jnp.concatenate([fields[strip, pl.ds(at, 16), :] for strip in range(STRIPS)], axis=0)
+
+    depth, along_u, along_v, sea = whole(0), whole(16), whole(32), whole(48)
+    above = lambda v: jnp.concatenate([v[1:], v[:1]], axis=0)
+    beyond = lambda v: jnp.where(lane == TALL - 1, 0.0, pltpu.roll(v, TALL - 1, 1))
+    step_x = small_ref[pl.ds(4, 1), :]
+    half_x = 0.5 * step_x * sea * above(sea)
+    half_y = 0.5 * (TIME_STEP / CELL_SIZE) * sea * beyond(sea)
+
+    def spread(ref, at, value):
+        for x in range(WIDE):
+            ref[at, x] = jnp.broadcast_to(value[x : x + 1, :], (8, TALL))
+
+    spread(drift, 0, half_x * (along_u + above(along_u)))
+    spread(drift, 1, half_y * (along_v + beyond(along_v)))
+    for which in range(4):
+        frequency = small_ref[pl.ds(which, 1), :]
+        angular = 2.0 * math.pi * frequency
+        deep_number = angular * angular / GRAVITY
+        wavenumber = deep_number / jnp.sqrt(jnp.tanh(deep_number * depth))
+        relative = jnp.minimum(wavenumber * depth, KH_LIMIT)
+        sinh = 0.5 * (jnp.exp(2.0 * relative) - jnp.exp(-2.0 * relative))
+        speed = (0.5 + relative / sinh) * angular / wavenumber
+        spread(first_rate, which, half_x * (speed + above(speed)))
+        spread(second_rate, which, half_y * (speed + beyond(speed)))
+
+    pieces = lax.shift_right_logical(lax.broadcasted_iota(jnp.int32, (1, 256), 1), 5)
+    base = me * ROWS
+    first_index = base // ND
+    row8 = lax.broadcasted_iota(jnp.int32, (8, TALL), 0)
+    wide_lane = lax.broadcasted_iota(jnp.int32, (WIDE * 8, TALL), 1)
+
+    def back(part, number, where):
+        at, rows = PARTS[part]
+        return remote(
+            leaving.at[number, pl.ds(at, rows)],
+            out_ref.at[pl.ds(aligned(me * ROWS + at), rows)],
+            back_send.at[part, number], back_recv.at[part, me], where,
+        )
+
+    def back_landed(part, number, where):
+        at, rows = PARTS[part]
+        spot = out_ref.at[pl.ds(aligned(number * ROWS + at), rows)]
+        return remote(spot, spot, back_send.at[part, number], back_recv.at[part, number], where)
+
+    def back_extra(number, where):
+        return remote(
+            leaving.at[number, pl.ds(ROWS, EXTRA)], out_ref.at[pl.ds(GROUP * ROWS, EXTRA)],
+            back_extra_send.at[number], back_extra_recv, where,
+        )
+
+    for part in range(len(PARTS)):
+        at, rows = PARTS[part]
+        for number, where in partners:
+            go_landed(part, number, where).wait_recv()
+        if part == 1:
+
+            @pl.when(me == LAST)
+            def _():
+                for number, where in partners:
+                    spot = arrived.at[number, pl.ds(ROWS, EXTRA)]
+                    remote(spot, spot, go_extra_send, go_extra_recv.at[number], where).wait_recv()
+
+        for strip in range(STRIPS):
+            blocks = [
+                arrived[strip * OWNERS + o, pl.ds(at, PART_ROWS), :].astype(jnp.float32)
+                for o in range(OWNERS)
+            ]
+            blocks = butterfly(blocks, pieces)
+            lined = []
+            for xx in range(TS):
+                block = blocks[-xx % 8]
+                if xx:
+                    block = pltpu.roll(block, 256 - 32 * xx, 1)
+                lined.append(block.astype(jnp.bfloat16))
+            placed = jnp.dot(
+                jnp.concatenate(lined, axis=0), tile_map[strip], preferred_element_type=jnp.float32
+            )
+            for xx in range(TS):
+                for half in range(2):
+                    density[strip * 16 + half * TS + xx] = placed[
+                        xx * PART_ROWS : (xx + 1) * PART_ROWS, half * TALL : (half + 1) * TALL
+                    ]
+
+        def chunk(step, carry):
+            start = base + at + step * 8
+            index = start // ND
+            table = index - first_index
+            later = jnp.minimum(table + 1, 3)
+            new = row8 >= (index + 1) * ND - start
+            here = pl.ds(pl.multiple_of(step * 8, 8), 8)
+            angle_at = pl.ds(pl.multiple_of(at + step * 8, 8), 8)
+            cos, sin = angle_ref[0, angle_at, :], angle_ref[1, angle_at, :]
+            face_x = jnp.where(new[None], first_rate[later], first_rate[table]) * cos[None] + drift[0]
+            face_y = jnp.where(new[None], second_rate[later], second_rate[table]) * sin[None] + drift[1]
+            bend_x = (1.0 - face_x * face_x) * (1.0 / 6.0)
+            bend_y = (1.0 - face_y * face_y) * (1.0 / 6.0)
+            d = density[:, here, :]
+            for substep in range(NSUB):
+                d = first_sweep(d, face_x, bend_x)
+                d = second_sweep(d, face_y, bend_y, wide_lane)
+            density[:, here, :] = d
+            return carry
+
+        count = PART_ROWS // 8 if part == 0 else jnp.where(me == LAST, PART_ROWS // 8, rows // 8)
+        lax.fori_loop(0, count, chunk, 0)
+
+        for strip in range(STRIPS):
+            lined = [
+                jnp.concatenate(
+                    [density[strip * 16 + xx], density[strip * 16 + TS + xx]], axis=1
+                ).astype(jnp.bfloat16)
+                for xx in range(TS)
+            ]
+            sorted_rows = lax.dot_general(
+                jnp.concatenate(lined, axis=0), tile_map[strip], (((1,), (1,)), ((), ())),
+                preferred_element_type=jnp.float32,
+            )
+            blocks = []
+            for xx in range(TS):
+                block = sorted_rows[xx * PART_ROWS : (xx + 1) * PART_ROWS]
+                blocks.append(pltpu.roll(block, 32 * xx, 1) if xx else block)
+            blocks = butterfly(blocks, pieces)
+            for o in range(OWNERS):
+                leaving[strip * OWNERS + o, pl.ds(at, PART_ROWS)] = blocks[-o % 8].astype(jnp.bfloat16)
+
+        for number, where in partners:
+            back(part, number, where).start()
+        if part == 1:
+
+            @pl.when(me == LAST)
+            def _():
+                for number, where in partners:
+                    back_extra(number, where).start()
+
+    out_ref[pl.ds(aligned(me * ROWS), ROWS), :] = leaving[me, pl.ds(0, ROWS), :]
+
+    @pl.when(me == LAST)
+    def _():
+        out_ref[pl.ds(GROUP * ROWS, EXTRA), :] = leaving[LAST, pl.ds(ROWS, EXTRA), :]
+
+    for part in range(len(PARTS)):
+        for number, where in partners:
+            go(part, number, where).wait_send()
+            back(part, number, where).wait_send()
+            back_landed(part, number, where).wait_recv()
+
+    @pl.when(me != LAST)
+    def _():
+        go_extra().wait_send()
+        spot = out_ref.at[pl.ds(GROUP * ROWS, EXTRA)]
+        remote(spot, spot, back_extra_send.at[LAST], back_extra_recv, final_device).wait_recv()
+
+    @pl.when(me == LAST)
+    def _():
+        for number, where in partners:
+            back_extra(number, where).wait_send()
+
+
+def exchange(source, place, field, small, angle):
+    dma = pltpu.SemaphoreType.DMA
+    vmem = pl.BlockSpec(memory_space=pltpu.VMEM)
+    return pl.pallas_call(
+        exchange_kernel,
+        out_shape=jax.ShapeDtypeStruct((K, 256), jnp.bfloat16),
+        in_specs=[vmem] * 5,
+        out_specs=vmem,
+        scratch_shapes=[
+            pltpu.VMEM((K, 256), jnp.bfloat16),
+            pltpu.VMEM((GROUP, CAP, 256), jnp.bfloat16),
+            pltpu.VMEM((STRIPS, FIELD_ROWS, TALL), jnp.float32),
+            pltpu.VMEM((WIDE, PART_ROWS, TALL), jnp.float32),
+            pltpu.VMEM((GROUP, CAP, 256), jnp.bfloat16),
+            pltpu.VMEM((4, WIDE, 8, TALL), jnp.float32),
+            pltpu.VMEM((4, WIDE, 8, TALL), jnp.float32),
+            pltpu.VMEM((2, WIDE, 8, TALL), jnp.float32),
+            pltpu.VMEM((STRIPS, 256, 256), jnp.bfloat16),
+            dma((2, GROUP)), dma((2, GROUP)), dma, dma((GROUP,)),
+            dma((2, GROUP)), dma((2, GROUP)), dma((GROUP,)), dma, dma, dma,
+        ],
+        compiler_params=pltpu.CompilerParams(
+            collective_id=0, has_side_effects=True, vmem_limit_bytes=40 * 1024 * 1024
+        ),
+    )(source, place, field, small, angle)
+
+
+def grouped(
+    spectrum, wind_speed, wind_dir, freq_kernel, dir_kernel, depth, current, land_mask, tile_owner
+):
+    owner = lax.axis_index("comp") * lax.axis_size("sub") + lax.axis_index("sub")
+    me = lax.axis_index("tile") * OWNERS + owner
+    owners = tile_owner[0]
+    tile_cells = (
+        land_mask.reshape(2, TS, TALL // TS, TS).transpose(0, 2, 1, 3).reshape(32, 64)
+    ).astype(jnp.float32)
+    number = jnp.arange(32)
+    same_before = (owners[None, :] == owners[:, None]) & (number[None, :] < number[:, None])
+    rank = jnp.sum(same_before.astype(jnp.int32), axis=1)
+    chosen = ((owners[None, :] == owner) & (rank[None, :] == jnp.arange(RANKS)[:, None])).astype(
+        jnp.float32
+    )
+    mine = (chosen @ tile_cells).reshape(RANKS * 64)
+    spot = jnp.arange(256)
+    before = (spot[:, None] < spot[None, :]).astype(jnp.float32)
+    slot = (mine[None, :] @ before)[0]
+    slot = jnp.where(mine > 0.5, slot, -1.0)
+    slot = slot.reshape(RANKS, TS, TS).transpose(1, 0, 2)
+    slot = jnp.roll(slot, owner, axis=0).reshape(256)
+    place = (slot[None, :] == spot.astype(jnp.float32)[:, None]).astype(jnp.bfloat16)
+    target = (owners * 32 + rank * TS)[:, None] + jnp.arange(TS)[None, :]
+    target = jnp.pad(target.reshape(2, TALL).astype(jnp.float32), ((0, 6), (0, 0)))
+    field = jnp.concatenate(
+        [depth, current[0], current[1], land_mask.astype(jnp.float32), target], axis=0
+    )
+    component = me * ROWS + jnp.arange(CAP)
+    angles = directions(ND)[component % ND]
+    angle = jnp.broadcast_to(
+        jnp.stack([jnp.cos(angles), jnp.sin(angles)])[:, :, None], (2, CAP, TALL)
+    )
+    index = jnp.minimum((me * ROWS) // ND + jnp.arange(4), NF - 1)
+    small = jnp.concatenate(
+        [
+            jnp.broadcast_to(frequencies(NF)[index][:, None], (4, TALL)),
+            (TIME_STEP / (CELL_SIZE * row_metric(TALL)))[None],
+            jnp.zeros((3, TALL), jnp.float32),
+        ],
+        axis=0,
+    )
+    source = source_terms(spectrum[0, 0], wind_speed[0, 0], wind_dir[0, 0], freq_kernel, dir_kernel)
+    returned = exchange(source, place, field, small, angle)
+    result = lax.dot_general(
+        returned, place, (((1,), (1,)), ((), ())), preferred_element_type=jnp.float32
+    ).astype(jnp.bfloat16)
+    return result.reshape(1, 1, K, PCAP)
+
+
 def solution(mesh):
+    sizes = mesh.shape
+    fits = (sizes["comp"], sizes["sub"], sizes["tile"]) == (4, 2, STRIPS)
     placed = (
         P(("ens", "tile"), ("comp", "sub"), None, None),
         P(("ens", "tile"), ("comp", "sub"), None),
@@ -226,7 +608,7 @@
         P("tile", None),
     )
     return jax.shard_map(
-        local,
+        grouped if fits else local,
         mesh=mesh,
         in_specs=placed,
         out_specs=P(("ens", "tile"), ("comp", "sub"), None, None),

time: 131 us -> 53 us (0.40)
  Pallas kernels: 0 us -> 40 us
  local copies, waits for them, and re-layouts: 44.2 us -> 4.83 us
  waiting for transfers between devices: 23.7 us -> 0 us
  blocking collectives: 23 us -> 0 us
  other arithmetic: 22.3 us -> 1.89 us
  starting transfers between devices: 12.6 us -> 0 us
  matrix products: 3.24 us -> 5.02 us
    pallas_call x0 -> x1, Pallas kernels: none -> 40 us  [exchange(): pl.pallas_call(exchange_kernel, out_shape=jax.ShapeDtypeStruct((K, 256),...]
    ppermute x6 -> x0, waiting for transfers between devices: 23.7 us -> none  [the longest x3 14.2 us: padded(): before = lax.ppermute(last, axis, up)]
    all_to_all x1 -> x0, blocking collectives: 23 us -> none  [local(): lax.all_to_all(picked, ('comp', 'sub'), split_axis=1, concat_axis=0, tile...]
    gather x5 -> x2, local copies, waits for them, and re-layouts: 21 us -> 1.87 us  [the longest x1 1.23 us: grouped(): angles = directions(ND)[component % ND]]
    scatter x2 -> x0, local copies, waits for them, and re-layouts: 16.3 us -> none  [the longest x1 8.23 us: layout_maps(): jnp.zeros((owner_count * PCAP,), jnp.int32).at[targets]]
    mul x8 -> x2, other arithmetic: 9.47 us -> 0.02 us  [grouped(): target = (owners * 32 + rank * TS)[:, None] + jnp.arange(TS)[None, :]]
    ppermute x6 -> x0, starting transfers between devices: 7.26 us -> none  [the longest x3 6.12 us: padded(): before = lax.ppermute(last, axis, up)]
    div x3 -> x1, other arithmetic: 5.54 us -> 0.05 us  [grouped(): TIME_STEP / (CELL_SIZE * row_metric(TALL))]
  transfers between devices with their start and end apart: 7 -> 0, of which waited for: 4 -> 0; matrix products, arithmetic and copies ran while one was open for 26% -> 0% of each run, Pallas kernels for 0% -> 0%
where the time goes in v1:
time: 53 us; the launch traced here: 52.8 us
  Pallas kernels  40 us (75%)
  matrix products  5.02 us (9%)
  local copies, waits for them, and re-layouts  4.83 us (9%)
  other arithmetic  1.89 us (4%)
  between operations  1.07 us (2%)
    pallas_call x1, Pallas kernels, exchange(): pl.pallas_call(exchange_kernel, out_shape=jax.ShapeDtypeStruct((K, 256),...  40 us
    dot_general x1, matrix products, source_terms(): jnp.einsum('cj,ajp->acp', dir_kernel, coupled, precision=lax.Precision.HI...  2.48 us
    dot_general x1, matrix products, grouped(): lax.dot_general(returned, place, (((1,), (1,)), ((), ())), preferred_elem...  1.29 us
    gather x1, local copies, waits for them, and re-layouts, grouped(): angles = directions(ND)[component % ND]  1.23 us
    squeeze x1, local copies, waits for them, and re-layouts, grouped(): spectrum[0, 0]  1.22 us

profile of v1, /device:TPU:0, one launch (start us, length us, event | category | flops | bytes accessed | tf_op | source)
XLA Modules:
  0.0 52.8 jit_solution(17736457855803598627)
XLA Ops:
  0.0 0.0 copy-start
  0.0 1.2 %squeeze.11 = bf16[36,36,256]{2,1,0:T(8,128)(2,1)S(1)} reshape(bf16[1,1,1296,256]{3,2,1,0:T(8,128)(2,1)} %param.9) | data formatting | bytes 1327104 | tf_op jit(solution)/shard_map/squeeze | solution.py:588
  1.2 0.0 copy-done
  1.2 0.0 copy-start.4
  1.3 0.0 copy-start.5
  1.3 0.0 copy-start.6
  1.3 0.7 %fusion.10 = f32[36,36,256]{2,0,1:T(8,128)S(1)} fusion(bf16[36,36,256]{2,1,0:T(8,128)(2,1)S(1)} %squeeze.11, f32[36,36]{1,0:T(8,128)S(1)} %copy-done), kind=kOutput, calls=%fused_computation.15 | convolution fusion | flops 143327232 | bytes 1995840 | tf_op jit(solution)/shard_map/ab,bjp->ajp/dot_general | solution.py:92
  2.0 0.2 convert_reduce_fusion
  2.2 0.1 multiply_reduce_fusion
  2.3 0.6 %fusion.31 = f32[]{:T(128)} fusion(), kind=kLoop, calls=%fused_computation.75 | loop fusion | flops 107 | bytes 4 | tf_op jit(solution)/shard_map/reduce_sum | solution.py:77
  3.6 0.0 copy-done.4
  3.6 0.2 fusion.15
  3.8 0.0 copy-done.5
  3.9 0.1 broadcast_divide_fusion
  3.9 0.0 copy-done.6
  3.9 2.5 %fusion.7 = bf16[36,36,256]{2,1,0:T(8,128)(2,1)S(1)} fusion(bf16[36,36,256]{2,1,0:T(8,128)(2,1)S(1)} %squeeze.11, f32[36,36,256]{2,0,1:T(8,128)S(1)} %fusion.10, f32[36,256]{1,0:T(8,128)S(1)} %get-tuple-element.14, f32[256]{0:T(256)S(1)} %get-tuple-element.8, f32[36,256]{1,0:T(8,128)S(1)} %get-tuple-element.15, f32[36,256]{1,0:T(8,128)S(1)} %broadcast_divide_fusion, ...), kind=kOutput, calls=%fused_computation.14 | convolution fusion | flops 147640320 | bytes 2771008 | tf_op jit(solution)/shard_map/cj,ajp->acp/dot_general | solution.py:93
  6.4 0.0 copy-start.1
  6.4 0.0 copy-start.7
  6.5 0.0 copy-start.3
  6.5 0.0 copy-start.2
  6.5 0.1 convert_element_type.97.source_ref
  6.6 0.1 lt.105
  6.7 0.1 iota_compare_fusion
  6.9 0.3 copy-done.1
  7.1 0.1 convert_element_type.100
  7.3 0.1 copy.14
  7.4 0.1 convert_element_type.102
  7.5 0.0 copy-done.7
  7.5 0.2 convert_reduce_fusion.1
  7.7 0.1 broadcast_compare_fusion
  7.8 0.1 reshape.348
  7.9 0.4 fusion.26
  8.3 0.1 gt.12
  8.4 0.1 eq.63
  8.5 0.1 compare_convert_fusion.place_ref
  8.6 0.0 copy-done.3
  8.7 0.0 copy-done.2
  8.7 0.1 mul.190
  8.8 0.1 mul.193
  8.9 0.1 add.174
  9.0 0.1 add.175
  9.1 0.1 add.177
  9.2 0.1 multiply_divide_fusion
  9.3 0.1 pad.9.clone
  9.4 0.6 %gather_fusion = f32[4]{0:T(128)S(1)} fusion(f32[36]{0:T(128)S(1)} %fusion.30, s32[1024]{0:T(1024)S(1)} %get-tuple-element.17), kind=kCustom, calls=%fused_computation | custom fusion | bytes 48 | tf_op jit(solution)/shard_map/gather | solution.py:582
  10.0 0.1 maximum_maximum_fusion.small_ref
  10.1 1.2 %gather_fusion.1 = f32[96]{0:T(128)S(1)} fusion(f32[36]{0:T(128)S(1)} %add_multiply_fusion, s32[1024]{0:T(1024)S(1)} %get-tuple-element.16), kind=kCustom, calls=%fused_computation.1 | custom fusion | bytes 1152 | tf_op jit(solution)/shard_map/gather | solution.py:575
  11.4 0.1 broadcast_in_dim.13.angle_ref
  11.5 40.0 %shard_map.91 = bf16[1296,256]{1,0:T(8,128)(2,1)S(1)} custom-call(bf16[1296,256]{1,0:T(8,128)(2,1)S(1)} %convert_element_type.97.source_ref, bf16[256,256]{1,0:T(8,128)(2,1)S(1)} %compare_convert_fusion.place_ref, f32[72,128]{1,0:T(8,128)S(1)} %constant_dynamic-update-slice_fusion.field_ref, f32[8,128]{1,0:T(8,128)S(1)} %maximum_maximum_fusion.small_ref, ...), custom_call_target="tpu_custom_call" | custom-call | tf_op jit(solution)/shard_map/pallas_call | solution.py:522
  51.5 1.3 %fusion = bf16[1,1,1296,256]{3,2,1,0:T(8,128)(2,1)} fusion(bf16[1296,256]{1,0:T(8,128)(2,1)S(1)} %shard_map.91, f32[256]{0:T(256)S(1)} %eq.63, f32[256]{0:T(256)S(1)} %iota_convert_fusion), kind=kOutput, calls=%fused_computation.7 | convolution fusion | flops 170266624 | bytes 1329152 | tf_op jit(solution)/shard_map/dot_general | solution.py:590
  (27 shorter events, 0.3 us)
Async XLA Ops:
  0.0 1.2 %copy-start = (f32[36,36]{1,0:T(8,128)S(1)}, f32[36,36]{1,0:T(8,128)}, u32[]{:S(2)}) copy-start(f32[36,36]{1,0:T(8,128)} %param.12) | copy-start | bytes 15556
  1.2 2.4 %copy-start.4 = (f32[1,1,256]{2,1,0:T(1,128)S(1)}, f32[1,1,256]{2,1,0:T(1,128)}, u32[]{:S(2)}) copy-start(f32[1,1,256]{2,1,0:T(1,128)} %param.11) | copy-start | bytes 3076
  1.3 2.6 %copy-start.5 = (f32[1,1,256]{2,1,0:T(1,128)S(1)}, f32[1,1,256]{2,1,0:T(1,128)}, u32[]{:S(2)}) copy-start(f32[1,1,256]{2,1,0:T(1,128)} %param.10) | copy-start | bytes 3076
  1.3 2.7 %copy-start.6 = (f32[36,36]{1,0:T(8,128)S(1)}, f32[36,36]{1,0:T(8,128)}, u32[]{:S(2)}) copy-start(f32[36,36]{1,0:T(8,128)} %param.13) | copy-start | bytes 15556
  6.4 0.7 %copy-start.1 = (s32[16,128]{1,0:T(8,128)S(1)}, s32[16,128]{1,0:T(8,128)}, u32[]{:S(2)}) copy-start(s32[16,128]{1,0:T(8,128)} %param.16) | copy-start | bytes 24580
  6.4 1.0 %copy-start.7 = (s32[1,32]{1,0:T(1,128)S(1)}, s32[1,32]{1,0:T(1,128)}, u32[]{:S(2)}) copy-start(s32[1,32]{1,0:T(1,128)} %param.17) | copy-start | bytes 388
  6.5 2.2 %copy-start.3 = (f32[16,128]{1,0:T(8,128)S(1)}, f32[16,128]{1,0:T(8,128)}, u32[]{:S(2)}) copy-start(f32[16,128]{1,0:T(8,128)} %param.14) | copy-start | bytes 24580
  6.5 2.2 %copy-start.2 = (f32[2,16,128]{2,1,0:T(8,128)S(1)}, f32[2,16,128]{2,1,0:T(8,128)}, u32[]{:S(2)}) copy-start(f32[2,16,128]{2,1,0:T(8,128)} %param.15) | copy-start | bytes 49156

commit v2 on v1

--- a/solution.py
+++ b/solution.py
@@ -89,8 +89,8 @@
         * (frequency[:, None, None] / mean_freq[None, None, :])
         * jnp.square(mean_energy / ENERGY_REF)[None, None, :]
     )
-    coupled = jnp.einsum("ab,bjp->ajp", freq_kernel, energy, precision=lax.Precision.HIGHEST)
-    coupled = jnp.einsum("cj,ajp->acp", dir_kernel, coupled, precision=lax.Precision.HIGHEST)
+    coupled = jnp.einsum("ab,bjp->ajp", freq_kernel, energy, precision=lax.Precision.HIGH)
+    coupled = jnp.einsum("cj,ajp->acp", dir_kernel, coupled, precision=lax.Precision.HIGH)
     transfer = TRANSFER_RATE * energy * coupled / mean_energy[None, None, :]
     updated = (energy + growth * energy + transfer) / (1.0 + damping)
     return updated.reshape(freq_count * dir_count, points).astype(jnp.bfloat16)
@@ -267,8 +267,9 @@
 
 
 def exchange_kernel(
-    source_ref, place_ref, field_ref, small_ref, angle_ref, out_ref,
+    source_ref, depth_ref, current_ref, mask_ref, owner_ref, out_ref, place_ref,
     packed, arrived, fields, density, leaving, first_rate, second_rate, drift, tile_map,
+    field_ref, angle_ref,
     go_send, go_recv, go_extra_send, go_extra_recv,
     back_send, back_recv, back_extra_send, back_extra_recv, field_send, field_recv,
 ):
@@ -295,9 +296,58 @@
             device_id=where, device_id_type=pl.DeviceIdType.MESH,
         )
 
+    def iota(shape, dim):
+        return lax.broadcasted_iota(jnp.int32, shape, dim)
+
+    def number(condition):
+        return jnp.where(condition, 1.0, 0.0)
+
+    tiles = 2 * TALL // TS
+    owners = owner_ref[...].astype(jnp.float32)
+    owner_rows = jnp.broadcast_to(owners, (tiles, tiles))
+    eye = iota((tiles, tiles), 0) == iota((tiles, tiles), 1)
+    owner_column = jnp.sum(jnp.where(eye, owner_rows, 0.0), axis=1, keepdims=True)
+    earlier = (owner_column == owner_rows) & (iota((tiles, tiles), 0) < iota((tiles, tiles), 1))
+    rank = jnp.sum(number(earlier), axis=0, keepdims=True)
+    column = iota((tiles, 256), 1)
+    spread_tile = number(lax.shift_right_logical(column, 3) == iota((tiles, 256), 0))
+    target = jnp.dot(owners * 32.0 + rank * 8.0, spread_tile, preferred_element_type=jnp.float32)
+    target = target + (iota((1, 256), 1) & 7).astype(jnp.float32)
+    field_ref[pl.ds(0, 16), :] = depth_ref[...]
+    field_ref[pl.ds(16, 16), :] = current_ref[0]
+    field_ref[pl.ds(32, 16), :] = current_ref[1]
+    field_ref[pl.ds(48, 16), :] = mask_ref[...].astype(jnp.float32)
+    field_ref[pl.ds(64, 1), :] = target[:, :TALL]
+    field_ref[pl.ds(65, 1), :] = target[:, TALL:]
+    field_ref[pl.ds(66, 6), :] = jnp.zeros((6, TALL), jnp.float32)
     beside = partner(0, 1, 0)[1]
     field_copy = remote(field_ref, fields.at[tile], field_send, field_recv, beside)
     field_copy.start()
+
+    mine_owner = comp * 2 + sub
+    wanted = (owner_column == mine_owner.astype(jnp.float32))
+    rank_column = jnp.sum(jnp.where(eye, jnp.broadcast_to(rank, (tiles, tiles)), 0.0), axis=1, keepdims=True)
+    lane_rank = lax.shift_right_logical(iota((1, 256), 1), 3) & 3
+    held = wanted & (rank_column == lane_rank.astype(jnp.float32))
+    tile_of = jnp.sum(jnp.where(held, iota((tiles, 256), 0).astype(jnp.float32), 0.0), axis=0, keepdims=True)
+    tile_of = tile_of.astype(jnp.int32)
+
+    def cell_x(at):
+        return (lax.shift_right_logical(at, 5) - mine_owner) & 7
+
+    def order(at):
+        return (lax.shift_right_logical(at, 3) & 3) * 64 + cell_x(at) * 8 + (at & 7)
+
+    lanes = iota((1, 256), 1)
+    column_y = (tile_of & 15) * 8 + (lanes & 7)
+    column_x = lax.shift_right_logical(tile_of, 4) * 8 + cell_x(lanes)
+    pick = number(iota((TALL, 256), 0) == column_y)
+    by_x = jnp.dot(mask_ref[...].astype(jnp.float32), pick, preferred_element_type=jnp.float32)
+    mine = jnp.sum(jnp.where(iota((16, 256), 0) == column_x, by_x, 0.0), axis=0, keepdims=True)
+    before = number(order(iota((256, 256), 0)) < order(iota((256, 256), 1)))
+    slot = jnp.dot(jnp.broadcast_to(mine, (8, 256)), before, preferred_element_type=jnp.float32)[:1]
+    slot = jnp.where(mine > 0.5, slot, -1.0).astype(jnp.int32)
+    place_ref[...] = number(iota((256, 256), 0) == slot).astype(jnp.bfloat16)
 
     packed[...] = jnp.dot(
         source_ref[...], place_ref[...], preferred_element_type=jnp.float32
@@ -362,7 +412,8 @@
     depth, along_u, along_v, sea = whole(0), whole(16), whole(32), whole(48)
     above = lambda v: jnp.concatenate([v[1:], v[:1]], axis=0)
     beyond = lambda v: jnp.where(lane == TALL - 1, 0.0, pltpu.roll(v, TALL - 1, 1))
-    step_x = small_ref[pl.ds(4, 1), :]
+    latitude = LAT_EDGE * (2.0 * (lane.astype(jnp.float32) + 0.5) / TALL - 1.0)
+    step_x = TIME_STEP / (CELL_SIZE * jnp.cos(latitude))
     half_x = 0.5 * step_x * sea * above(sea)
     half_y = 0.5 * (TIME_STEP / CELL_SIZE) * sea * beyond(sea)
 
@@ -372,8 +423,17 @@
 
     spread(drift, 0, half_x * (along_u + above(along_u)))
     spread(drift, 1, half_y * (along_v + beyond(along_v)))
+    base = me * ROWS
+    first_index = base // ND
+    component = base + iota((CAP, TALL), 0)
+    direction = component - ND * lax.shift_right_logical(component * 1821, 16)
+    angle = (2.0 * math.pi / ND) * (direction.astype(jnp.float32) + 0.5)
+    angle_ref[0] = jnp.cos(angle)
+    angle_ref[1] = jnp.sin(angle)
     for which in range(4):
-        frequency = small_ref[pl.ds(which, 1), :]
+        index = jnp.minimum(first_index + which, NF - 1).astype(jnp.float32)
+        exponent = jnp.broadcast_to(index * math.log(FREQ_RATIO), (1, TALL))
+        frequency = FREQ_BASE * jnp.exp(exponent)
         angular = 2.0 * math.pi * frequency
         deep_number = angular * angular / GRAVITY
         wavenumber = deep_number / jnp.sqrt(jnp.tanh(deep_number * depth))
@@ -384,8 +444,6 @@
         spread(second_rate, which, half_y * (speed + beyond(speed)))
 
     pieces = lax.shift_right_logical(lax.broadcasted_iota(jnp.int32, (1, 256), 1), 5)
-    base = me * ROWS
-    first_index = base // ND
     row8 = lax.broadcasted_iota(jnp.int32, (8, TALL), 0)
     wide_lane = lax.broadcasted_iota(jnp.int32, (WIDE * 8, TALL), 1)
 
@@ -516,14 +574,17 @@
             back_extra(number, where).wait_send()
 
 
-def exchange(source, place, field, small, angle):
+def exchange(source, depth, current, land_mask, tile_owner):
     dma = pltpu.SemaphoreType.DMA
     vmem = pl.BlockSpec(memory_space=pltpu.VMEM)
     return pl.pallas_call(
         exchange_kernel,
-        out_shape=jax.ShapeDtypeStruct((K, 256), jnp.bfloat16),
+        out_shape=[
+            jax.ShapeDtypeStruct((K, 256), jnp.bfloat16),
+            jax.ShapeDtypeStruct((256, 256), jnp.bfloat16),
+        ],
         in_specs=[vmem] * 5,
-        out_specs=vmem,
+        out_specs=[vmem] * 2,
         scratch_shapes=[
             pltpu.VMEM((K, 256), jnp.bfloat16),
             pltpu.VMEM((GROUP, CAP, 256), jnp.bfloat16),
@@ -534,59 +595,22 @@
             pltpu.VMEM((4, WIDE, 8, TALL), jnp.float32),
             pltpu.VMEM((2, WIDE, 8, TALL), jnp.float32),
             pltpu.VMEM((STRIPS, 256, 256), jnp.bfloat16),
+            pltpu.VMEM((FIELD_ROWS, TALL), jnp.float32),
+            pltpu.VMEM((2, CAP, TALL), jnp.float32),
             dma((2, GROUP)), dma((2, GROUP)), dma, dma((GROUP,)),
             dma((2, GROUP)), dma((2, GROUP)), dma((GROUP,)), dma, dma, dma,
         ],
         compiler_params=pltpu.CompilerParams(
             collective_id=0, has_side_effects=True, vmem_limit_bytes=40 * 1024 * 1024
         ),
-    )(source, place, field, small, angle)
+    )(source, depth, current, land_mask, tile_owner)
 
 
 def grouped(
     spectrum, wind_speed, wind_dir, freq_kernel, dir_kernel, depth, current, land_mask, tile_owner
 ):
-    owner = lax.axis_index("comp") * lax.axis_size("sub") + lax.axis_index("sub")
-    me = lax.axis_index("tile") * OWNERS + owner
-    owners = tile_owner[0]
-    tile_cells = (
-        land_mask.reshape(2, TS, TALL // TS, TS).transpose(0, 2, 1, 3).reshape(32, 64)
-    ).astype(jnp.float32)
-    number = jnp.arange(32)
-    same_before = (owners[None, :] == owners[:, None]) & (number[None, :] < number[:, None])
-    rank = jnp.sum(same_before.astype(jnp.int32), axis=1)
-    chosen = ((owners[None, :] == owner) & (rank[None, :] == jnp.arange(RANKS)[:, None])).astype(
-        jnp.float32
-    )
-    mine = (chosen @ tile_cells).reshape(RANKS * 64)
-    spot = jnp.arange(256)
-    before = (spot[:, None] < spot[None, :]).astype(jnp.float32)
-    slot = (mine[None, :] @ before)[0]
-    slot = jnp.where(mine > 0.5, slot, -1.0)
-    slot = slot.reshape(RANKS, TS, TS).transpose(1, 0, 2)
-    slot = jnp.roll(slot, owner, axis=0).reshape(256)
-    place = (slot[None, :] == spot.astype(jnp.float32)[:, None]).astype(jnp.bfloat16)
-    target = (owners * 32 + rank * TS)[:, None] + jnp.arange(TS)[None, :]
-    target = jnp.pad(target.reshape(2, TALL).astype(jnp.float32), ((0, 6), (0, 0)))
-    field = jnp.concatenate(
-        [depth, current[0], current[1], land_mask.astype(jnp.float32), target], axis=0
-    )
-    component = me * ROWS + jnp.arange(CAP)
-    angles = directions(ND)[component % ND]
-    angle = jnp.broadcast_to(
-        jnp.stack([jnp.cos(angles), jnp.sin(angles)])[:, :, None], (2, CAP, TALL)
-    )
-    index = jnp.minimum((me * ROWS) // ND + jnp.arange(4), NF - 1)
-    small = jnp.concatenate(
-        [
-            jnp.broadcast_to(frequencies(NF)[index][:, None], (4, TALL)),
-            (TIME_STEP / (CELL_SIZE * row_metric(TALL)))[None],
-            jnp.zeros((3, TALL), jnp.float32),
-        ],
-        axis=0,
-    )
     source = source_terms(spectrum[0, 0], wind_speed[0, 0], wind_dir[0, 0], freq_kernel, dir_kernel)
-    returned = exchange(source, place, field, small, angle)
+    returned, place = exchange(source, depth, current, land_mask, tile_owner)
     result = lax.dot_general(
         returned, place, (((1,), (1,)), ((), ())), preferred_element_type=jnp.float32
     ).astype(jnp.bfloat16)

time: 53 us -> 48.2 us (0.909)
  local copies, waits for them, and re-layouts: 4.83 us -> 1.38 us
  matrix products: 5.02 us -> 3.55 us
    gather x2 -> x0, local copies, waits for them, and re-layouts: 1.87 us -> none  [the longest x1 1.23 us: grouped(): angles = directions(ND)[component % ND]]
    dot_general x4 -> x2, matrix products: 3.74 us -> 2.34 us  [the longest x1 1.79 us: source_terms(): jnp.einsum('cj,ajp->acp', dir_kernel, coupled, precision=lax.Precision.HIGH)]
    div x1, other arithmetic: 0.08 us -> 0.76 us  [source_terms(): wind_speed[None, None, :] / phase_speed[:, None, None]]
where the time goes in v2:
time: 48.2 us; the launch traced here: 48 us
  Pallas kernels  40.4 us (84%)
  matrix products  3.55 us (7%)
  other arithmetic  1.88 us (4%)
  local copies, waits for them, and re-layouts  1.38 us (3%)
  between operations  0.83 us (2%)
    pallas_call x1, Pallas kernels, exchange(): pl.pallas_call(exchange_kernel, out_shape=[jax.ShapeDtypeStruct((K, 256),...  40.4 us
    dot_general x1, matrix products, source_terms(): jnp.einsum('cj,ajp->acp', dir_kernel, coupled, precision=lax.Precision.HIGH)  1.79 us
    squeeze x1, local copies, waits for them, and re-layouts, grouped(): spectrum[0, 0]  1.22 us
    dot_general x1, matrix products, grouped(): lax.dot_general(returned, place, (((1,), (1,)), ((), ())), preferred_elem...  1.21 us

profile of v2, /device:TPU:0, one launch (start us, length us, event | category | flops | bytes accessed | tf_op | source)
XLA Modules:
  0.0 48.0 jit_solution(11422691101577596574)
XLA Ops:
  0.0 0.0 copy-start
  0.0 0.0 copy-start.5
  0.0 0.6 %fusion.16 = f32[]{:T(128)} fusion(), kind=kLoop, calls=%fused_computation.29 | loop fusion | flops 107 | bytes 4 | tf_op jit(solution)/shard_map/reduce_sum | solution.py:77
  1.3 0.8 %broadcast_divide_fusion = f32[36,256]{1,0:T(8,128)S(1)} fusion(f32[36]{0:T(128)S(1)} %multiply_divide_fusion, f32[256]{0:T(256)} %bitcast.19), kind=kLoop, calls=%fused_computation.22 | loop fusion | flops 9216 | bytes 38032 | tf_op jit(solution)/shard_map/div | solution.py:81
  2.1 1.2 %squeeze.3 = bf16[36,36,256]{2,1,0:T(8,128)(2,1)S(1)} reshape(bf16[1,1,1296,256]{3,2,1,0:T(8,128)(2,1)} %param.9) | data formatting | bytes 1327104 | tf_op jit(solution)/shard_map/squeeze | solution.py:612
  3.3 0.0 copy-start.6
  3.3 0.2 convert_reduce_fusion
  3.5 0.1 multiply_reduce_fusion
  3.6 0.0 copy-done.5
  3.6 0.2 fusion.12
  3.8 0.0 copy-done
  3.8 0.5 %fusion.10 = f32[36,36,256]{2,0,1:T(8,128)S(1)} fusion(bf16[36,36,256]{2,1,0:T(8,128)(2,1)S(1)} %squeeze.3, f32[36,36]{1,0:T(8,128)S(1)} %copy-done), kind=kOutput, calls=%fused_computation.13 | convolution fusion | flops 71663616 | bytes 1995840 | tf_op jit(solution)/shard_map/ab,bjp->ajp/dot_general | solution.py:92
  4.4 0.0 copy-done.6
  4.4 0.0 copy-start.1
  4.4 0.0 copy-start.2
  4.4 0.0 copy-start.3
  4.4 0.0 copy-start.4
  4.4 1.8 %fusion.7 = bf16[36,36,256]{2,1,0:T(8,128)(2,1)S(1)} fusion(bf16[36,36,256]{2,1,0:T(8,128)(2,1)S(1)} %squeeze.3, f32[36,36,256]{2,0,1:T(8,128)S(1)} %fusion.10, f32[36,256]{1,0:T(8,128)S(1)} %get-tuple-element.14, f32[256]{0:T(256)S(1)} %get-tuple-element.12, f32[36,256]{1,0:T(8,128)S(1)} %get-tuple-element.15, f32[36,256]{1,0:T(8,128)S(1)} %broadcast_divide_fusion, ...), kind=kOutput, calls=%fused_computation.12 | convolution fusion | flops 75976704 | bytes 2771008 | tf_op jit(solution)/shard_map/cj,ajp->acp/dot_general | solution.py:93
  6.2 0.1 convert_element_type.48.source_ref
  6.4 0.0 copy-done.1
  6.4 0.0 copy-done.2
  6.4 0.0 copy-done.3
  6.4 0.0 copy-done.4
  6.4 40.4 %shard_map.91 = (bf16[1296,256]{1,0:T(8,128)(2,1)S(1)}, bf16[256,256]{1,0:T(8,128)(2,1)S(1)}) custom-call(bf16[1296,256]{1,0:T(8,128)(2,1)S(1)} %convert_element_type.48.source_ref, f32[16,128]{1,0:T(8,128)S(1)} %copy-done.2, f32[2,16,128]{2,1,0:T(8,128)S(1)} %copy-done.1, s32[16,128]{1,0:T(8,128)S(1)} %copy-done.3, s32[1,32]{1,0:T(1,128)S(1)} %copy-done.4), custom_call_target="tpu_custom_call" | custom-call | tf_op jit(solution)/shard_map/pallas_call | solution.py:580
  46.8 1.2 %fusion = bf16[1,1,1296,256]{3,2,1,0:T(8,128)(2,1)} fusion(bf16[1296,256]{1,0:T(8,128)(2,1)S(1)} %get-tuple-element.7, bf16[256,256]{1,0:T(8,128)(2,1)S(1)} %get-tuple-element.8), kind=kOutput, calls=%fused_computation.5 | convolution fusion | flops 170201088 | bytes 1458176 | tf_op jit(solution)/shard_map/dot_general | solution.py:614
  (4 shorter events, 0.0 us)
Async XLA Ops:
  0.0 3.8 %copy-start = (f32[36,36]{1,0:T(8,128)S(1)}, f32[36,36]{1,0:T(8,128)}, u32[]{:S(2)}) copy-start(f32[36,36]{1,0:T(8,128)} %param.12) | copy-start | bytes 15556
  0.0 3.6 %copy-start.5 = (f32[1,1,256]{2,1,0:T(1,128)S(1)}, f32[1,1,256]{2,1,0:T(1,128)}, u32[]{:S(2)}) copy-start(f32[1,1,256]{2,1,0:T(1,128)} %param.11) | copy-start | bytes 3076
  3.3 1.1 %copy-start.6 = (f32[36,36]{1,0:T(8,128)S(1)}, f32[36,36]{1,0:T(8,128)}, u32[]{:S(2)}) copy-start(f32[36,36]{1,0:T(8,128)} %param.13) | copy-start | bytes 15556
  4.4 2.0 %copy-start.1 = (f32[2,16,128]{2,1,0:T(8,128)S(1)}, f32[2,16,128]{2,1,0:T(8,128)}, u32[]{:S(2)}) copy-start(f32[2,16,128]{2,1,0:T(8,128)} %current_ref.1) | copy-start | bytes 49156
  4.4 2.0 %copy-start.2 = (f32[16,128]{1,0:T(8,128)S(1)}, f32[16,128]{1,0:T(8,128)}, u32[]{:S(2)}) copy-start(f32[16,128]{1,0:T(8,128)} %depth_ref.1) | copy-start | bytes 24580
  4.4 2.0 %copy-start.3 = (s32[16,128]{1,0:T(8,128)S(1)}, s32[16,128]{1,0:T(8,128)}, u32[]{:S(2)}) copy-start(s32[16,128]{1,0:T(8,128)} %mask_ref.1) | copy-start | bytes 24580
  4.4 2.0 %copy-start.4 = (s32[1,32]{1,0:T(1,128)S(1)}, s32[1,32]{1,0:T(1,128)}, u32[]{:S(2)}) copy-start(s32[1,32]{1,0:T(1,128)} %owner_ref.1) | copy-start | bytes 388

commit v3 on v2

--- a/solution.py
+++ b/solution.py
@@ -74,13 +74,17 @@
     angles = directions(dir_count)
     weighted = jnp.sum(energy, axis=1) * frequency[:, None]
     first_moment = jnp.sum(weighted, axis=0)
-    mean_energy = first_moment / (dir_count * jnp.sum(frequency))
+    total = FREQ_BASE * sum(FREQ_RATIO**i for i in range(freq_count))
+    mean_energy = first_moment / (dir_count * total)
     mean_freq = jnp.sum(weighted * frequency[:, None], axis=0) / first_moment
     phase_speed = GRAVITY / (2.0 * math.pi * frequency)
     forcing = (
         wind_speed[None, None, :]
         / phase_speed[:, None, None]
-        * jnp.cos(angles[None, :, None] - heading[None, None, :])
+        * (
+            jnp.cos(angles)[None, :, None] * jnp.cos(heading)[None, None, :]
+            + jnp.sin(angles)[None, :, None] * jnp.sin(heading)[None, None, :]
+        )
         - 1.0
     )
     growth = WIND_RATE * jnp.maximum(forcing, 0.0)
@@ -223,8 +227,9 @@
 EXTRA = 16
 CAP = ROWS + EXTRA
 LAST = GROUP - 1
-PARTS = ((0, 48), (48, 32))
-PART_ROWS = 48
+PARTS = ((0, 32), (32, 32), (64, 16))
+FINAL = len(PARTS) - 1
+MOST_ROWS = max(PARTS[FINAL][1] + EXTRA, *(rows for _, rows in PARTS))
 WIDE = 32
 TALL = 128
 FIELD_ROWS = 72
@@ -468,9 +473,10 @@
 
     for part in range(len(PARTS)):
         at, rows = PARTS[part]
+        height = rows + EXTRA if part == FINAL else rows
         for number, where in partners:
             go_landed(part, number, where).wait_recv()
-        if part == 1:
+        if part == FINAL:
 
             @pl.when(me == LAST)
             def _():
@@ -480,7 +486,7 @@
 
         for strip in range(STRIPS):
             blocks = [
-                arrived[strip * OWNERS + o, pl.ds(at, PART_ROWS), :].astype(jnp.float32)
+                arrived[strip * OWNERS + o, pl.ds(at, height), :].astype(jnp.float32)
                 for o in range(OWNERS)
             ]
             blocks = butterfly(blocks, pieces)
@@ -495,8 +501,8 @@
             )
             for xx in range(TS):
                 for half in range(2):
-                    density[strip * 16 + half * TS + xx] = placed[
-                        xx * PART_ROWS : (xx + 1) * PART_ROWS, half * TALL : (half + 1) * TALL
+                    density[strip * 16 + half * TS + xx, pl.ds(0, height)] = placed[
+                        xx * height : (xx + 1) * height, half * TALL : (half + 1) * TALL
                     ]
 
         def chunk(step, carry):
@@ -519,13 +525,13 @@
             density[:, here, :] = d
             return carry
 
-        count = PART_ROWS // 8 if part == 0 else jnp.where(me == LAST, PART_ROWS // 8, rows // 8)
+        count = rows // 8 if part < FINAL else jnp.where(me == LAST, height // 8, rows // 8)
         lax.fori_loop(0, count, chunk, 0)
 
         for strip in range(STRIPS):
             lined = [
                 jnp.concatenate(
-                    [density[strip * 16 + xx], density[strip * 16 + TS + xx]], axis=1
+                    [density[strip * 16 + half * TS + xx, pl.ds(0, height)] for half in range(2)], axis=1
                 ).astype(jnp.bfloat16)
                 for xx in range(TS)
             ]
@@ -535,15 +541,15 @@
             )
             blocks = []
             for xx in range(TS):
-                block = sorted_rows[xx * PART_ROWS : (xx + 1) * PART_ROWS]
+                block = sorted_rows[xx * height : (xx + 1) * height]
                 blocks.append(pltpu.roll(block, 32 * xx, 1) if xx else block)
             blocks = butterfly(blocks, pieces)
             for o in range(OWNERS):
-                leaving[strip * OWNERS + o, pl.ds(at, PART_ROWS)] = blocks[-o % 8].astype(jnp.bfloat16)
+                leaving[strip * OWNERS + o, pl.ds(at, height)] = blocks[-o % 8].astype(jnp.bfloat16)
 
         for number, where in partners:
             back(part, number, where).start()
-        if part == 1:
+        if part == FINAL:
 
             @pl.when(me == LAST)
             def _():
@@ -589,7 +595,7 @@
             pltpu.VMEM((K, 256), jnp.bfloat16),
             pltpu.VMEM((GROUP, CAP, 256), jnp.bfloat16),
             pltpu.VMEM((STRIPS, FIELD_ROWS, TALL), jnp.float32),
-            pltpu.VMEM((WIDE, PART_ROWS, TALL), jnp.float32),
+            pltpu.VMEM((WIDE, MOST_ROWS, TALL), jnp.float32),
             pltpu.VMEM((GROUP, CAP, 256), jnp.bfloat16),
             pltpu.VMEM((4, WIDE, 8, TALL), jnp.float32),
             pltpu.VMEM((4, WIDE, 8, TALL), jnp.float32),
@@ -597,8 +603,8 @@
             pltpu.VMEM((STRIPS, 256, 256), jnp.bfloat16),
             pltpu.VMEM((FIELD_ROWS, TALL), jnp.float32),
             pltpu.VMEM((2, CAP, TALL), jnp.float32),
-            dma((2, GROUP)), dma((2, GROUP)), dma, dma((GROUP,)),
-            dma((2, GROUP)), dma((2, GROUP)), dma((GROUP,)), dma, dma, dma,
+            dma((len(PARTS), GROUP)), dma((len(PARTS), GROUP)), dma, dma((GROUP,)),
+            dma((len(PARTS), GROUP)), dma((len(PARTS), GROUP)), dma((GROUP,)), dma, dma, dma,
         ],
         compiler_params=pltpu.CompilerParams(
             collective_id=0, has_side_effects=True, vmem_limit_bytes=40 * 1024 * 1024

time: 48.2 us -> 45.7 us (0.948)
  other arithmetic: 1.88 us -> 0.49 us
  Pallas kernels: 40.4 us -> 39.2 us
  local copies, waits for them, and re-layouts: 1.38 us -> 2.11 us
  between operations: 0.83 us -> 0.17 us
    pallas_call x1, Pallas kernels: 40.4 us -> 39.2 us  [exchange(): pl.pallas_call(exchange_kernel, out_shape=[jax.ShapeDtypeStruct((K, 256),...]
    div x2 -> x1, other arithmetic: 0.76 us -> 0.01 us  [source_terms(): mean_energy = first_moment / (dir_count * total)]
    cos x0 -> x1, local copies, waits for them, and re-layouts: none -> 0.73 us  [source_terms(): jnp.cos(heading)[None, None, :]]
    reduce_sum x1 -> x0, other arithmetic: 0.61 us -> none  [source_terms(): mean_energy = first_moment / (dir_count * jnp.sum(frequency))]
where the time goes in v3:
time: 45.7 us; the launch traced here: 45.5 us
  Pallas kernels  39.2 us (86%)
  matrix products  3.55 us (8%)
  local copies, waits for them, and re-layouts  2.11 us (5%)
  other arithmetic  0.49 us (1%)
    pallas_call x1, Pallas kernels, exchange(): pl.pallas_call(exchange_kernel, out_shape=[jax.ShapeDtypeStruct((K, 256),...  39.2 us
    dot_general x1, matrix products, source_terms(): jnp.einsum('cj,ajp->acp', dir_kernel, coupled, precision=lax.Precision.HIGH)  1.79 us
    squeeze x1, local copies, waits for them, and re-layouts, grouped(): spectrum[0, 0]  1.22 us
    dot_general x1, matrix products, grouped(): lax.dot_general(returned, place, (((1,), (1,)), ((), ())), preferred_elem...  1.21 us

profile of v3, /device:TPU:0, one launch (start us, length us, event | category | flops | bytes accessed | tf_op | source)
XLA Modules:
  0.0 45.5 jit_solution(728995330140073275)
XLA Ops:
  0.0 0.0 copy-start
  0.0 0.0 copy-start.5
  0.1 0.7 %fusion.18 = (f32[1,1,256]{2,1,0:T(1,128)S(1)}, f32[1,1,256]{2,1,0:T(1,128)S(1)}) fusion(f32[1,1,256]{2,1,0:T(1,128)} %param.11), kind=kLoop, calls=%fused_computation.31 | loop fusion | bytes 3072 | tf_op jit(solution)/shard_map/cos | solution.py:85
  0.8 0.1 multiply_add_fusion
  0.9 1.2 %squeeze.4 = bf16[36,36,256]{2,1,0:T(8,128)(2,1)S(1)} reshape(bf16[1,1,1296,256]{3,2,1,0:T(8,128)(2,1)} %param.9) | data formatting | bytes 1327104 | tf_op jit(solution)/shard_map/squeeze | solution.py:618
  2.1 0.0 copy-start.6
  2.1 0.2 convert_reduce_fusion
  2.3 0.1 multiply_reduce_fusion
  2.4 0.0 copy-done.5
  2.4 0.1 fusion.12
  2.5 0.0 copy-done
  2.5 0.5 %fusion.10 = f32[36,36,256]{2,0,1:T(8,128)S(1)} fusion(bf16[36,36,256]{2,1,0:T(8,128)(2,1)S(1)} %squeeze.4, f32[36,36]{1,0:T(8,128)S(1)} %copy-done), kind=kOutput, calls=%fused_computation.13 | convolution fusion | flops 71663616 | bytes 1995840 | tf_op jit(solution)/shard_map/ab,bjp->ajp/dot_general | solution.py:96
  3.1 0.0 copy-done.6
  3.1 0.0 copy-start.1
  3.1 0.0 copy-start.2
  3.1 0.0 copy-start.3
  3.1 0.0 copy-start.4
  3.1 1.8 %fusion.7 = bf16[36,36,256]{2,1,0:T(8,128)(2,1)S(1)} fusion(bf16[36,36,256]{2,1,0:T(8,128)(2,1)S(1)} %squeeze.4, f32[36,36,256]{2,0,1:T(8,128)S(1)} %fusion.10, f32[36,256]{1,0:T(8,128)S(1)} %get-tuple-element.18, f32[256]{0:T(256)S(1)} %get-tuple-element.13, f32[36,256]{1,0:T(8,128)S(1)} %multiply_add_fusion, f32[36,256]{1,0:T(8,128)S(1)} %get-tuple-element.19, ...), kind=kOutput, calls=%fused_computation.12 | convolution fusion | flops 75976704 | bytes 2771008 | tf_op jit(solution)/shard_map/cj,ajp->acp/dot_general | solution.py:97
  4.9 0.1 convert_element_type.51.source_ref
  5.1 0.0 copy-done.1
  5.1 0.0 copy-done.2
  5.1 0.0 copy-done.3
  5.1 0.0 copy-done.4
  5.1 39.2 %shard_map.91 = (bf16[1296,256]{1,0:T(8,128)(2,1)S(1)}, bf16[256,256]{1,0:T(8,128)(2,1)S(1)}) custom-call(bf16[1296,256]{1,0:T(8,128)(2,1)S(1)} %convert_element_type.51.source_ref, f32[16,128]{1,0:T(8,128)S(1)} %copy-done.2, f32[2,16,128]{2,1,0:T(8,128)S(1)} %copy-done.1, s32[16,128]{1,0:T(8,128)S(1)} %copy-done.3, s32[1,32]{1,0:T(1,128)S(1)} %copy-done.4), custom_call_target="tpu_custom_call" | custom-call | tf_op jit(solution)/shard_map/pallas_call | solution.py:586
  44.3 1.2 %fusion = bf16[1,1,1296,256]{3,2,1,0:T(8,128)(2,1)} fusion(bf16[1296,256]{1,0:T(8,128)(2,1)S(1)} %get-tuple-element.7, bf16[256,256]{1,0:T(8,128)(2,1)S(1)} %get-tuple-element.8), kind=kOutput, calls=%fused_computation.5 | convolution fusion | flops 170201088 | bytes 1458176 | tf_op jit(solution)/shard_map/dot_general | solution.py:620
  (4 shorter events, 0.1 us)
Async XLA Ops:
  0.0 2.5 %copy-start = (f32[36,36]{1,0:T(8,128)S(1)}, f32[36,36]{1,0:T(8,128)}, u32[]{:S(2)}) copy-start(f32[36,36]{1,0:T(8,128)} %param.12) | copy-start | bytes 15556
  0.0 2.4 %copy-start.5 = (f32[1,1,256]{2,1,0:T(1,128)S(1)}, f32[1,1,256]{2,1,0:T(1,128)}, u32[]{:S(2)}) copy-start(f32[1,1,256]{2,1,0:T(1,128)} %param.10) | copy-start | bytes 3076
  2.1 1.0 %copy-start.6 = (f32[36,36]{1,0:T(8,128)S(1)}, f32[36,36]{1,0:T(8,128)}, u32[]{:S(2)}) copy-start(f32[36,36]{1,0:T(8,128)} %param.13) | copy-start | bytes 15556
  3.1 2.0 %copy-start.1 = (f32[2,16,128]{2,1,0:T(8,128)S(1)}, f32[2,16,128]{2,1,0:T(8,128)}, u32[]{:S(2)}) copy-start(f32[2,16,128]{2,1,0:T(8,128)} %current_ref.1) | copy-start | bytes 49156
  3.1 2.0 %copy-start.2 = (f32[16,128]{1,0:T(8,128)S(1)}, f32[16,128]{1,0:T(8,128)}, u32[]{:S(2)}) copy-start(f32[16,128]{1,0:T(8,128)} %depth_ref.1) | copy-start | bytes 24580
  3.1 2.0 %copy-start.3 = (s32[16,128]{1,0:T(8,128)S(1)}, s32[16,128]{1,0:T(8,128)}, u32[]{:S(2)}) copy-start(s32[16,128]{1,0:T(8,128)} %mask_ref.1) | copy-start | bytes 24580
  3.1 2.0 %copy-start.4 = (s32[1,32]{1,0:T(1,128)S(1)}, s32[1,32]{1,0:T(1,128)}, u32[]{:S(2)}) copy-start(s32[1,32]{1,0:T(1,128)} %owner_ref.1) | copy-start | bytes 388

commit v4 on v3

--- a/solution.py
+++ b/solution.py
@@ -63,6 +63,18 @@
     relative = jnp.minimum(wavenumber * sea_depth, KH_LIMIT)
     group_ratio = 0.5 + relative / jnp.sinh(2.0 * relative)
     return group_ratio * angular / wavenumber
+
+
+def heading_parts(heading):
+    quarter = 0.25 * heading
+    square = quarter * quarter
+    sine = 1.0 / 5040.0 - square / 362880.0
+    sine = quarter * (1.0 - square * (1.0 / 6.0 - square * (1.0 / 120.0 - square * sine)))
+    cosine = 1.0 / 720.0 - square * (1.0 / 40320.0 - square / 3628800.0)
+    cosine = 1.0 - square * (0.5 - square * (1.0 / 24.0 - square * cosine))
+    for _ in range(2):
+        sine, cosine = 2.0 * sine * cosine, 1.0 - 2.0 * sine * sine
+    return cosine, sine
 
 
 def source_terms(spectrum_block, wind_speed, heading, freq_kernel, dir_kernel):
@@ -78,12 +90,13 @@
     mean_energy = first_moment / (dir_count * total)
     mean_freq = jnp.sum(weighted * frequency[:, None], axis=0) / first_moment
     phase_speed = GRAVITY / (2.0 * math.pi * frequency)
+    heading_cos, heading_sin = heading_parts(heading)
     forcing = (
         wind_speed[None, None, :]
         / phase_speed[:, None, None]
         * (
-            jnp.cos(angles)[None, :, None] * jnp.cos(heading)[None, None, :]
-            + jnp.sin(angles)[None, :, None] * jnp.sin(heading)[None, None, :]
+            jnp.cos(angles)[None, :, None] * heading_cos[None, None, :]
+            + jnp.sin(angles)[None, :, None] * heading_sin[None, None, :]
         )
         - 1.0
     )
@@ -293,7 +306,6 @@
     barrier = pltpu.get_barrier_semaphore()
     for _, where in partners:
         pl.semaphore_signal(barrier, inc=1, device_id=where, device_id_type=pl.DeviceIdType.MESH)
-    pl.semaphore_wait(barrier, GROUP - 1)
 
     def remote(src, dst, send, recv, where):
         return pltpu.make_async_remote_copy(
@@ -327,7 +339,6 @@
     field_ref[pl.ds(66, 6), :] = jnp.zeros((6, TALL), jnp.float32)
     beside = partner(0, 1, 0)[1]
     field_copy = remote(field_ref, fields.at[tile], field_send, field_recv, beside)
-    field_copy.start()
 
     mine_owner = comp * 2 + sub
     wanted = (owner_column == mine_owner.astype(jnp.float32))
@@ -357,6 +368,9 @@
     packed[...] = jnp.dot(
         source_ref[...], place_ref[...], preferred_element_type=jnp.float32
     ).astype(jnp.bfloat16)
+
+    pl.semaphore_wait(barrier, GROUP - 1)
+    field_copy.start()
 
     def aligned(value):
         return pl.multiple_of(value, 16)

time: 45.7 us -> 44.6 us (0.976)
  Pallas kernels: 39.2 us -> 38.1 us
  local copies, waits for them, and re-layouts: 2.11 us -> 1.38 us
  other arithmetic: 0.49 us -> 1.2 us
    pallas_call x1, Pallas kernels: 39.2 us -> 38.1 us  [exchange(): pl.pallas_call(exchange_kernel, out_shape=[jax.ShapeDtypeStruct((K, 256),...]
    cos x1 -> x0, local copies, waits for them, and re-layouts: 0.73 us -> none  [source_terms(): jnp.cos(heading)[None, None, :]]
    sub x0 -> x1, other arithmetic: none -> 0.7 us  [heading_parts(): sine, cosine = (2.0 * sine * cosine, 1.0 - 2.0 * sine * sine)]
where the time goes in v4:
time: 44.6 us; the launch traced here: 44.4 us
  Pallas kernels  38.1 us (85%)
  matrix products  3.55 us (8%)
  local copies, waits for them, and re-layouts  1.38 us (3%)
  other arithmetic  1.2 us (3%)
    pallas_call x1, Pallas kernels, exchange(): pl.pallas_call(exchange_kernel, out_shape=[jax.ShapeDtypeStruct((K, 256),...  38.1 us
    dot_general x1, matrix products, source_terms(): jnp.einsum('cj,ajp->acp', dir_kernel, coupled, precision=lax.Precision.HIGH)  1.79 us
    squeeze x1, local copies, waits for them, and re-layouts, grouped(): spectrum[0, 0]  1.22 us
    dot_general x1, matrix products, grouped(): lax.dot_general(returned, place, (((1,), (1,)), ((), ())), preferred_elem...  1.21 us

profile of v4, /device:TPU:0, one launch (start us, length us, event | category | flops | bytes accessed | tf_op | source)
XLA Modules:
  0.0 44.4 jit_solution(16117798070801033008)
XLA Ops:
  0.0 0.0 copy-start
  0.0 0.0 copy-start.5
  0.1 0.7 %fusion.16 = (f32[1,1,256]{2,1,0:T(1,128)S(1)}, f32[1,1,256]{2,1,0:T(1,128)S(1)}, f32[1,1,256]{2,1,0:T(1,128)S(1)}) fusion(f32[1,1,256]{2,1,0:T(1,128)} %param.11), kind=kLoop, calls=%fused_computation.28 | loop fusion | flops 6656 | bytes 4096 | tf_op jit(solution)/shard_map/sub | solution.py:76
  0.8 0.1 multiply_add_fusion
  0.9 1.2 %squeeze.4 = bf16[36,36,256]{2,1,0:T(8,128)(2,1)S(1)} reshape(bf16[1,1,1296,256]{3,2,1,0:T(8,128)(2,1)} %param.9) | data formatting | bytes 1327104 | tf_op jit(solution)/shard_map/squeeze | solution.py:632
  2.1 0.0 copy-start.6
  2.1 0.2 convert_reduce_fusion
  2.3 0.1 multiply_reduce_fusion
  2.4 0.0 copy-done.5
  2.4 0.1 fusion.12
  2.5 0.0 copy-done
  2.5 0.5 %fusion.10 = f32[36,36,256]{2,0,1:T(8,128)S(1)} fusion(bf16[36,36,256]{2,1,0:T(8,128)(2,1)S(1)} %squeeze.4, f32[36,36]{1,0:T(8,128)S(1)} %copy-done), kind=kOutput, calls=%fused_computation.13 | convolution fusion | flops 71663616 | bytes 1995840 | tf_op jit(solution)/shard_map/ab,bjp->ajp/dot_general | solution.py:109
  3.1 0.0 copy-done.6
  3.1 0.0 copy-start.1
  3.1 0.0 copy-start.2
  3.1 0.0 copy-start.3
  3.1 0.0 copy-start.4
  3.1 1.8 %fusion.7 = bf16[36,36,256]{2,1,0:T(8,128)(2,1)S(1)} fusion(bf16[36,36,256]{2,1,0:T(8,128)(2,1)S(1)} %squeeze.4, f32[36,36,256]{2,0,1:T(8,128)S(1)} %fusion.10, f32[36,256]{1,0:T(8,128)S(1)} %get-tuple-element.19, f32[256]{0:T(256)S(1)} %get-tuple-element.14, f32[36,256]{1,0:T(8,128)S(1)} %multiply_add_fusion, f32[36,256]{1,0:T(8,128)S(1)} %get-tuple-element.20, ...), kind=kOutput, calls=%fused_computation.12 | convolution fusion | flops 75976704 | bytes 2771008 | tf_op jit(solution)/shard_map/cj,ajp->acp/dot_general | solution.py:110
  4.9 0.1 convert_element_type.51.source_ref
  5.0 0.0 copy-done.1
  5.1 0.0 copy-done.2
  5.1 0.0 copy-done.3
  5.1 0.0 copy-done.4
  5.1 38.1 %shard_map.91 = (bf16[1296,256]{1,0:T(8,128)(2,1)S(1)}, bf16[256,256]{1,0:T(8,128)(2,1)S(1)}) custom-call(bf16[1296,256]{1,0:T(8,128)(2,1)S(1)} %convert_element_type.51.source_ref, f32[16,128]{1,0:T(8,128)S(1)} %copy-done.2, f32[2,16,128]{2,1,0:T(8,128)S(1)} %copy-done.1, s32[16,128]{1,0:T(8,128)S(1)} %copy-done.3, s32[1,32]{1,0:T(1,128)S(1)} %copy-done.4), custom_call_target="tpu_custom_call" | custom-call | tf_op jit(solution)/shard_map/pallas_call | solution.py:600
  43.2 1.2 %fusion = bf16[1,1,1296,256]{3,2,1,0:T(8,128)(2,1)} fusion(bf16[1296,256]{1,0:T(8,128)(2,1)S(1)} %get-tuple-element.7, bf16[256,256]{1,0:T(8,128)(2,1)S(1)} %get-tuple-element.8), kind=kOutput, calls=%fused_computation.5 | convolution fusion | flops 170201088 | bytes 1458176 | tf_op jit(solution)/shard_map/dot_general | solution.py:634
  (5 shorter events, 0.1 us)
Async XLA Ops:
  0.0 2.5 %copy-start = (f32[36,36]{1,0:T(8,128)S(1)}, f32[36,36]{1,0:T(8,128)}, u32[]{:S(2)}) copy-start(f32[36,36]{1,0:T(8,128)} %param.12) | copy-start | bytes 15556
  0.0 2.4 %copy-start.5 = (f32[1,1,256]{2,1,0:T(1,128)S(1)}, f32[1,1,256]{2,1,0:T(1,128)}, u32[]{:S(2)}) copy-start(f32[1,1,256]{2,1,0:T(1,128)} %param.10) | copy-start | bytes 3076
  2.1 1.0 %copy-start.6 = (f32[36,36]{1,0:T(8,128)S(1)}, f32[36,36]{1,0:T(8,128)}, u32[]{:S(2)}) copy-start(f32[36,36]{1,0:T(8,128)} %param.13) | copy-start | bytes 15556
  3.1 2.0 %copy-start.1 = (f32[2,16,128]{2,1,0:T(8,128)S(1)}, f32[2,16,128]{2,1,0:T(8,128)}, u32[]{:S(2)}) copy-start(f32[2,16,128]{2,1,0:T(8,128)} %current_ref.1) | copy-start | bytes 49156
  3.1 2.0 %copy-start.2 = (f32[16,128]{1,0:T(8,128)S(1)}, f32[16,128]{1,0:T(8,128)}, u32[]{:S(2)}) copy-start(f32[16,128]{1,0:T(8,128)} %depth_ref.1) | copy-start | bytes 24580
  3.1 2.0 %copy-start.3 = (s32[16,128]{1,0:T(8,128)S(1)}, s32[16,128]{1,0:T(8,128)}, u32[]{:S(2)}) copy-start(s32[16,128]{1,0:T(8,128)} %mask_ref.1) | copy-start | bytes 24580
  3.1 2.0 %copy-start.4 = (s32[1,32]{1,0:T(1,128)S(1)}, s32[1,32]{1,0:T(1,128)}, u32[]{:S(2)}) copy-start(s32[1,32]{1,0:T(1,128)} %owner_ref.1) | copy-start | bytes 388

commit v5 on v4

--- a/solution.py
+++ b/solution.py
@@ -365,9 +365,20 @@
     slot = jnp.where(mine > 0.5, slot, -1.0).astype(jnp.int32)
     place_ref[...] = number(iota((256, 256), 0) == slot).astype(jnp.bfloat16)
 
-    packed[...] = jnp.dot(
-        source_ref[...], place_ref[...], preferred_element_type=jnp.float32
-    ).astype(jnp.bfloat16)
+    def pack(part):
+        at, rows = PARTS[part]
+        spans = [(group * ROWS + at, rows) for group in range(GROUP)]
+        if part == FINAL:
+            spans.append((GROUP * ROWS, EXTRA))
+        block = jnp.concatenate([source_ref[pl.ds(*span), :] for span in spans], axis=0)
+        block = jnp.dot(block, place_ref[...], preferred_element_type=jnp.float32)
+        block = block.astype(jnp.bfloat16)
+        done = 0
+        for start, size in spans:
+            packed[pl.ds(start, size), :] = block[done : done + size]
+            done += size
+
+    pack(0)
 
     pl.semaphore_wait(barrier, GROUP - 1)
     field_copy.start()
@@ -395,6 +406,8 @@
         )
 
     for part in range(len(PARTS)):
+        if part:
+            pack(part)
         for number, where in partners:
             go(part, number, where).start()
 

time: 44.6 us -> 44.7 us (level)
  no operation moved by 1% of the time
where the time goes in v5:
time: 44.7 us; the launch traced here: 44.5 us
  Pallas kernels  38.2 us (85%)
  matrix products  3.55 us (8%)
  local copies, waits for them, and re-layouts  1.38 us (3%)
  other arithmetic  1.2 us (3%)
    pallas_call x1, Pallas kernels, exchange(): pl.pallas_call(exchange_kernel, out_shape=[jax.ShapeDtypeStruct((K, 256),...  38.2 us
    dot_general x1, matrix products, source_terms(): jnp.einsum('cj,ajp->acp', dir_kernel, coupled, precision=lax.Precision.HIGH)  1.79 us
    squeeze x1, local copies, waits for them, and re-layouts, grouped(): spectrum[0, 0]  1.22 us
    dot_general x1, matrix products, grouped(): lax.dot_general(returned, place, (((1,), (1,)), ((), ())), preferred_elem...  1.21 us

profile of v5, /device:TPU:0, one launch (start us, length us, event | category | flops | bytes accessed | tf_op | source)
XLA Modules:
  0.0 44.5 jit_solution(13476968738024269229)
XLA Ops:
  0.0 0.0 copy-start
  0.0 0.0 copy-start.5
  0.1 0.7 %fusion.16 = (f32[1,1,256]{2,1,0:T(1,128)S(1)}, f32[1,1,256]{2,1,0:T(1,128)S(1)}, f32[1,1,256]{2,1,0:T(1,128)S(1)}) fusion(f32[1,1,256]{2,1,0:T(1,128)} %param.11), kind=kLoop, calls=%fused_computation.28 | loop fusion | flops 6656 | bytes 4096 | tf_op jit(solution)/shard_map/sub | solution.py:76
  0.8 0.1 multiply_add_fusion
  0.9 1.2 %squeeze.4 = bf16[36,36,256]{2,1,0:T(8,128)(2,1)S(1)} reshape(bf16[1,1,1296,256]{3,2,1,0:T(8,128)(2,1)} %param.9) | data formatting | bytes 1327104 | tf_op jit(solution)/shard_map/squeeze | solution.py:645
  2.1 0.0 copy-start.6
  2.1 0.2 convert_reduce_fusion
  2.3 0.1 multiply_reduce_fusion
  2.4 0.0 copy-done.5
  2.4 0.1 fusion.12
  2.5 0.0 copy-done
  2.5 0.5 %fusion.10 = f32[36,36,256]{2,0,1:T(8,128)S(1)} fusion(bf16[36,36,256]{2,1,0:T(8,128)(2,1)S(1)} %squeeze.4, f32[36,36]{1,0:T(8,128)S(1)} %copy-done), kind=kOutput, calls=%fused_computation.13 | convolution fusion | flops 71663616 | bytes 1995840 | tf_op jit(solution)/shard_map/ab,bjp->ajp/dot_general | solution.py:109
  3.1 0.0 copy-done.6
  3.1 0.0 copy-start.1
  3.1 0.0 copy-start.2
  3.1 0.0 copy-start.3
  3.1 0.0 copy-start.4
  3.1 1.8 %fusion.7 = bf16[36,36,256]{2,1,0:T(8,128)(2,1)S(1)} fusion(bf16[36,36,256]{2,1,0:T(8,128)(2,1)S(1)} %squeeze.4, f32[36,36,256]{2,0,1:T(8,128)S(1)} %fusion.10, f32[36,256]{1,0:T(8,128)S(1)} %get-tuple-element.19, f32[256]{0:T(256)S(1)} %get-tuple-element.14, f32[36,256]{1,0:T(8,128)S(1)} %multiply_add_fusion, f32[36,256]{1,0:T(8,128)S(1)} %get-tuple-element.20, ...), kind=kOutput, calls=%fused_computation.12 | convolution fusion | flops 75976704 | bytes 2771008 | tf_op jit(solution)/shard_map/cj,ajp->acp/dot_general | solution.py:110
  4.9 0.1 convert_element_type.51.source_ref
  5.0 0.0 copy-done.1
  5.1 0.0 copy-done.2
  5.1 0.0 copy-done.3
  5.1 0.0 copy-done.4
  5.1 38.2 %shard_map.91 = (bf16[1296,256]{1,0:T(8,128)(2,1)S(1)}, bf16[256,256]{1,0:T(8,128)(2,1)S(1)}) custom-call(bf16[1296,256]{1,0:T(8,128)(2,1)S(1)} %convert_element_type.51.source_ref, f32[16,128]{1,0:T(8,128)S(1)} %copy-done.2, f32[2,16,128]{2,1,0:T(8,128)S(1)} %copy-done.1, s32[16,128]{1,0:T(8,128)S(1)} %copy-done.3, s32[1,32]{1,0:T(1,128)S(1)} %copy-done.4), custom_call_target="tpu_custom_call" | custom-call | tf_op jit(solution)/shard_map/pallas_call | solution.py:613
  43.3 1.2 %fusion = bf16[1,1,1296,256]{3,2,1,0:T(8,128)(2,1)} fusion(bf16[1296,256]{1,0:T(8,128)(2,1)S(1)} %get-tuple-element.7, bf16[256,256]{1,0:T(8,128)(2,1)S(1)} %get-tuple-element.8), kind=kOutput, calls=%fused_computation.5 | convolution fusion | flops 170201088 | bytes 1458176 | tf_op jit(solution)/shard_map/dot_general | solution.py:647
  (5 shorter events, 0.1 us)
Async XLA Ops:
  0.0 2.5 %copy-start = (f32[36,36]{1,0:T(8,128)S(1)}, f32[36,36]{1,0:T(8,128)}, u32[]{:S(2)}) copy-start(f32[36,36]{1,0:T(8,128)} %param.12) | copy-start | bytes 15556
  0.0 2.4 %copy-start.5 = (f32[1,1,256]{2,1,0:T(1,128)S(1)}, f32[1,1,256]{2,1,0:T(1,128)}, u32[]{:S(2)}) copy-start(f32[1,1,256]{2,1,0:T(1,128)} %param.10) | copy-start | bytes 3076
  2.1 1.0 %copy-start.6 = (f32[36,36]{1,0:T(8,128)S(1)}, f32[36,36]{1,0:T(8,128)}, u32[]{:S(2)}) copy-start(f32[36,36]{1,0:T(8,128)} %param.13) | copy-start | bytes 15556
  3.1 2.0 %copy-start.1 = (f32[2,16,128]{2,1,0:T(8,128)S(1)}, f32[2,16,128]{2,1,0:T(8,128)}, u32[]{:S(2)}) copy-start(f32[2,16,128]{2,1,0:T(8,128)} %current_ref.1) | copy-start | bytes 49156
  3.1 2.0 %copy-start.2 = (f32[16,128]{1,0:T(8,128)S(1)}, f32[16,128]{1,0:T(8,128)}, u32[]{:S(2)}) copy-start(f32[16,128]{1,0:T(8,128)} %depth_ref.1) | copy-start | bytes 24580
  3.1 2.0 %copy-start.3 = (s32[16,128]{1,0:T(8,128)S(1)}, s32[16,128]{1,0:T(8,128)}, u32[]{:S(2)}) copy-start(s32[16,128]{1,0:T(8,128)} %mask_ref.1) | copy-start | bytes 24580
  3.1 2.0 %copy-start.4 = (s32[1,32]{1,0:T(1,128)S(1)}, s32[1,32]{1,0:T(1,128)}, u32[]{:S(2)}) copy-start(s32[1,32]{1,0:T(1,128)} %owner_ref.1) | copy-start | bytes 388
